TPU v7x, 128 devices: a whole 4x4x4 slice. The times are simulated.
128 devices in a mesh: ctx: 16 (over z, x), tensor: 8 (over y, core).
Axes of the slice: x: 4, y: 4, z: 4, core: 2. Of those that a mesh axis runs over, the one named last changes fastest.
Arguments:
- hidden: bfloat16 [2048, 8192], P('ctx', 'tensor'), may hold values from -6 to 6
- norm_gain: float32 [8192], replicated, may hold values from 0.1 to 1.9
- w_query: bfloat16 [8192, 8192], P(None, 'tensor'), may hold values from -0.0625 to 0.0625
- w_key: bfloat16 [8192, 1024], P(None, 'tensor'), may hold values from -0.0625 to 0.0625
- w_value: bfloat16 [8192, 1024], P(None, 'tensor'), may hold values from -0.0625 to 0.0625
- cache_keys: bfloat16 [16384, 1024], P('ctx', 'tensor'), may hold values from -600 to 600
- cache_values: bfloat16 [16384, 1024], P('ctx', 'tensor'), may hold values from -6 to 6
- cache_lengths: int32 [16], P('ctx'), may hold values from 1 to 1024, 12288 in all
Outputs:
- attention: bfloat16 [2048, 8192], P('ctx', 'tensor')
Inputs may be any that keep to these rules, and one draw needn't show every extreme that they name: `cache_lengths`: each shard's valid slots form a prefix of its cache; some shard is full.
All inputs are finite; a program needn't handle non-finite values.
Results may differ from a plain program's by a relative error of at most 0.02.
The roundings to bfloat16 on the way count: a program that leaves them out, or rounds other values in their place, can miss the bound.
Values may be sent and summed in bfloat16 or wider, within the bound.
A program may use at most 128 MiB of HBM per device.

v0:
```python
import jax
import jax.numpy as jnp
from jax import lax
from jax.sharding import PartitionSpec as P

HEAD_DIM = 128


def rotate(values, positions, head_dim):
    rows = values.shape[0]
    heads = values.shape[1] // head_dim
    shaped = values.reshape(rows, heads, head_dim)
    half = head_dim // 2
    freq = jnp.power(jnp.float32(500000.0), -(jnp.arange(half, dtype=jnp.float32) * 2.0 / head_dim))
    angle = positions.astype(jnp.float32)[:, None] * freq[None, :]
    cosine = jnp.cos(angle)[:, None, :]
    sine = jnp.sin(angle)[:, None, :]
    first = shaped[:, :, :half]
    second = shaped[:, :, half:]
    turned = jnp.concatenate(
        [first * cosine - second * sine, second * cosine + first * sine], axis=2
    )
    return turned.reshape(rows, heads * head_dim)


def attend(queries, keys, values, valid_len, own_start, ctx_len, head_dim, kv_heads):
    total = queries.shape[0]
    width = queries.shape[1]
    heads = width // head_dim
    group = heads // kv_heads
    block = 512
    count = total // block
    slots = keys.shape[0]
    key_heads = keys.reshape(slots, kv_heads, head_dim)
    value_heads = values.reshape(slots, kv_heads, head_dim)
    slot_ids = jnp.arange(slots, dtype=jnp.int32)
    scale = 1.0 / head_dim**0.5

    def one_block(index):
        begin = index * block
        rows_q = lax.dynamic_slice_in_dim(queries, begin, block, 0).reshape(
            block, kv_heads, group, head_dim
        )
        score = (
            jnp.einsum("bkgd,tkd->bkgt", rows_q, key_heads, preferred_element_type=jnp.float32)
            * scale
        )
        row_ids = begin + jnp.arange(block, dtype=jnp.int32)
        cached = (slot_ids < ctx_len) & (slot_ids < valid_len)
        own = (slot_ids >= ctx_len)[None, :] & (
            (own_start + slot_ids - ctx_len)[None, :] <= row_ids[:, None]
        )
        valid = cached[None, :] | own
        score = jnp.where(valid[:, None, None, :], score, jnp.float32(-1e30))
        top = jnp.max(score, axis=3, keepdims=True)
        prob = jnp.where(valid[:, None, None, :], jnp.exp(score - top), jnp.float32(0.0))
        total_p = jnp.sum(prob, axis=3)
        prob_low = prob.astype(jnp.bfloat16)
        out = jnp.einsum(
            "bkgt,tkd->bkgd", prob_low, value_heads, preferred_element_type=jnp.float32
        )
        part = (out / total_p[..., None]).astype(jnp.bfloat16).reshape(block, width)
        lse = (top[..., 0] + jnp.log(total_p)).reshape(block, heads)
        return (part, lse)

    parts, lses = lax.map(one_block, jnp.arange(count, dtype=jnp.int32))
    return (parts.reshape(total, width), lses.reshape(total, heads))


def local(hidden, norm_gain, w_query, w_key, w_value, cache_keys, cache_values, cache_lengths):
    head_dim = HEAD_DIM
    whole = lax.all_gather(hidden, "tensor", axis=1, tiled=True)
    wide = whole.astype(jnp.float32)
    normed = (
        wide * lax.rsqrt(jnp.mean(wide * wide, axis=1, keepdims=True) + 1e-05) * norm_gain[None, :]
    ).astype(jnp.bfloat16)
    shards = lax.axis_size("ctx")
    place = lax.axis_index("ctx")
    rows = whole.shape[0]
    ctx_len = cache_keys.shape[0]
    kv_width = cache_keys.shape[1]
    kv_heads = kv_width // head_dim
    own_start = place * rows
    positions = shards * ctx_len + own_start + jnp.arange(rows, dtype=jnp.int32)
    query = rotate(
        jnp.dot(normed, w_query, preferred_element_type=jnp.float32), positions, head_dim
    ).astype(jnp.bfloat16)
    own_keys = rotate(
        jnp.dot(normed, w_key, preferred_element_type=jnp.float32), positions, head_dim
    ).astype(jnp.bfloat16)
    own_values = jnp.dot(normed, w_value, preferred_element_type=jnp.float32).astype(jnp.bfloat16)
    width = query.shape[1]
    heads = width // head_dim
    all_queries = lax.all_gather(query, "ctx", axis=0, tiled=True)
    keys = jnp.concatenate([cache_keys, own_keys], axis=0)
    values = jnp.concatenate([cache_values, own_values], axis=0)
    part, lse = attend(
        all_queries, keys, values, cache_lengths[0], own_start, ctx_len, head_dim, kv_heads
    )
    came_out = lax.all_to_all(
        part.reshape(shards, rows, width), "ctx", split_axis=0, concat_axis=0, tiled=True
    )
    came_lse = lax.all_to_all(
        lse.reshape(shards, rows, heads), "ctx", split_axis=0, concat_axis=0, tiled=True
    )
    top = jnp.max(came_lse, axis=0)
    weights = jnp.exp(came_lse - top[None])
    numer = jnp.sum(
        came_out.astype(jnp.float32).reshape(shards, rows, heads, head_dim) * weights[..., None],
        axis=0,
    )
    denom = jnp.sum(weights, axis=0)
    result = (numer / denom[..., None]).reshape(rows, width).astype(jnp.bfloat16)
    return result


def solution(mesh):
    placed = (
        P("ctx", "tensor"),
        P(),
        P(None, "tensor"),
        P(None, "tensor"),
        P(None, "tensor"),
        P("ctx", "tensor"),
        P("ctx", "tensor"),
        P("ctx"),
    )
    return jax.shard_map(
        local, mesh=mesh, in_specs=placed, out_specs=P("ctx", "tensor"), check_vma=False
    )
```

profile of v0, /device:TPU:0, one launch (start us, length us, event | category | flops | bytes accessed | tf_op | source)
XLA Modules:
  0.0 276.4 jit_solution(10578706543137924970)
XLA Ops:
  7.7 29.1 %all-gather.3.cloned.1.call-done = bf16[128,8192]{1,0:T(8,128)(2,1)} async-done(((bf16[128,1024]{1,0:T(8,128)(2,1)}), bf16[128,8192]{1,0:T(8,128)(2,1)}) %all-gather.3.cloned.1.call-update) | async-done | bytes 2097168 | tf_op jit(solution)/shard_map/all_gather | solution.py:72
  38.8 8.8 %convolution_bitcast_fusion = f32[16,8,8,128]{3,1,2,0:T(8,128)S(1)} fusion(bf16[8192,1024]{1,0:T(8,128)(2,1)} %param.12, bf16[128,8192]{1,0:T(8,128)(2,1)} %all-gather.3.cloned.1.call-done, f32[8192]{0:T(1024)} %param.11, f32[128]{0:T(128)S(1)} %add_rsqrt_fusion), kind=kOutput, calls=%fused_computation.33 | convolution fusion | flops 2151677952 | bytes 19431936 | tf_op jit(solution)/shard_map/dot_general | solution.py:86
  49.3 2.7 convolution_bitcast_fusion.1
  52.4 3.0 %convolution_convert_fusion = bf16[128,128]{1,0:T(8,128)(2,1)S(1)} fusion(bf16[8192,128]{1,0:T(8,128)(2,1)} %param.14, bf16[128,8192]{1,0:T(8,128)(2,1)} %all-gather.3.cloned.1.call-done, f32[8192]{0:T(1024)S(1)} %copy-done.4, f32[128]{0:T(128)S(1)} %add_rsqrt_fusion), kind=kOutput, calls=%fused_computation.35 | convolution fusion | flops 272646144 | bytes 4260352 | tf_op jit(solution)/shard_map/dot_general | solution.py:91
  55.6 51.6 %all-gather.5.cloned.1.call-done = bf16[2048,1024]{0,1:T(8,128)(2,1)} async-done(((bf16[128,1024]{0,1:T(8,128)(2,1)}), bf16[2048,1024]{0,1:T(8,128)(2,1)}) %all-gather.5.cloned.1.call-update) | async-done | bytes 4194320 | tf_op jit(solution)/shard_map/all_gather | solution.py:94
  107.2 81.0 %while.16 = (s32[]{:T(128)}, bf16[4,512,1024]{2,1,0:T(8,128)(2,1)}, f32[4,512,8]{1,2,0:T(8,128)S(1)}, s32[]{:T(128)}, s32[]{:T(128)}, /*index=5*/s32[4]{0:T(128)...) while((s32[]{:T(128)}, bf16[4,512,1024]{2,1,0:T(8,128)(2,1)}, ...), condition=%wide.region_4.5_spmd.clone.clone, body=%wide.region_1.4_spmd.clone.clone.sunk | while | flops 2470644992 | bytes 68110544 | solution.py:66
  111.0 4.6 %fusion.49 = (f32[512,8]{0,1:T(8,128)S(1)}, f32[512,8,1152]{2,0,1:T(8,128)S(1)}) fusion(pred[512,1152]{1,0:T(8,128)(4,1)S(1)} %and_or_fusion.2, bf16[512,8,128]{0,2,1:T(8,128)(2,1)S(1)} %bitcast.97, bf16[1152,1,128]{2,0,1:T(8,128)(2,1)S(1)} %get-tuple-element.314), kind=kOutput, calls=%fused_computation.4.clone.1 | convolution fusion | flops 1222111232 | bytes 20824064 | tf_op jit(solution)/shard_map/while/body/eval_jaxpr/bkgd,tkd->bkgt/dot_general | solution.py:45
  115.6 5.2 %fusion.50 = f32[512,8]{0,1:T(8,128)S(1)} fusion(f32[512,8,1152]{2,0,1:T(8,128)S(1)} %get-tuple-element.279, f32[512,8]{0,1:T(8,128)S(1)} %get-tuple-element.280, pred[512,1152]{1,0:T(8,128)(4,1)S(1)} %and_or_fusion.2), kind=kLoop, calls=%fused_computation.5.clone.1 | loop fusion | flops 18870272 | bytes 19496960 | tf_op jit(solution)/shard_map/while/body/eval_jaxpr/reduce_sum | solution.py:57
  120.9 5.0 %fusion.51 = bf16[1,128,512,8]{2,1,3,0:T(8,128)(2,1)S(1)} fusion(f32[512,8,1152]{2,0,1:T(8,128)S(1)} %get-tuple-element.279, f32[512,8]{0,1:T(8,128)S(1)} %get-tuple-element.280, pred[512,1152]{1,0:T(8,128)(4,1)S(1)} %and_or_fusion.2, f32[512,8]{0,1:T(8,128)S(1)} %fusion.50, bf16[1152,1,128]{0,2,1:T(8,128)(2,1)S(1)} %get-tuple-element.315), kind=kOutput, calls=%fused_computation.12.clone.1 | convolution fusion | flops 1227882496 | bytes 20840448 | tf_op jit(solution)/shard_map/while/body/eval_jaxpr/bkgt,tkd->bkgd/dot_general | solution.py:59
  131.2 4.6 %fusion.49 = (f32[512,8]{0,1:T(8,128)S(1)}, f32[512,8,1152]{2,0,1:T(8,128)S(1)}) fusion(pred[512,1152]{1,0:T(8,128)(4,1)S(1)} %and_or_fusion.2, bf16[512,8,128]{0,2,1:T(8,128)(2,1)S(1)} %bitcast.97, bf16[1152,1,128]{2,0,1:T(8,128)(2,1)S(1)} %get-tuple-element.314), kind=kOutput, calls=%fused_computation.4.clone.1 | convolution fusion | flops 1222111232 | bytes 20824064 | tf_op jit(solution)/shard_map/while/body/eval_jaxpr/bkgd,tkd->bkgt/dot_general | solution.py:45
  135.8 5.2 %fusion.50 = f32[512,8]{0,1:T(8,128)S(1)} fusion(f32[512,8,1152]{2,0,1:T(8,128)S(1)} %get-tuple-element.279, f32[512,8]{0,1:T(8,128)S(1)} %get-tuple-element.280, pred[512,1152]{1,0:T(8,128)(4,1)S(1)} %and_or_fusion.2), kind=kLoop, calls=%fused_computation.5.clone.1 | loop fusion | flops 18870272 | bytes 19496960 | tf_op jit(solution)/shard_map/while/body/eval_jaxpr/reduce_sum | solution.py:57
  141.1 5.0 %fusion.51 = bf16[1,128,512,8]{2,1,3,0:T(8,128)(2,1)S(1)} fusion(f32[512,8,1152]{2,0,1:T(8,128)S(1)} %get-tuple-element.279, f32[512,8]{0,1:T(8,128)S(1)} %get-tuple-element.280, pred[512,1152]{1,0:T(8,128)(4,1)S(1)} %and_or_fusion.2, f32[512,8]{0,1:T(8,128)S(1)} %fusion.50, bf16[1152,1,128]{0,2,1:T(8,128)(2,1)S(1)} %get-tuple-element.315), kind=kOutput, calls=%fused_computation.12.clone.1 | convolution fusion | flops 1227882496 | bytes 20840448 | tf_op jit(solution)/shard_map/while/body/eval_jaxpr/bkgt,tkd->bkgd/dot_general | solution.py:59
  151.5 4.6 %fusion.49 = (f32[512,8]{0,1:T(8,128)S(1)}, f32[512,8,1152]{2,0,1:T(8,128)S(1)}) fusion(pred[512,1152]{1,0:T(8,128)(4,1)S(1)} %and_or_fusion.2, bf16[512,8,128]{0,2,1:T(8,128)(2,1)S(1)} %bitcast.97, bf16[1152,1,128]{2,0,1:T(8,128)(2,1)S(1)} %get-tuple-element.314), kind=kOutput, calls=%fused_computation.4.clone.1 | convolution fusion | flops 1222111232 | bytes 20824064 | tf_op jit(solution)/shard_map/while/body/eval_jaxpr/bkgd,tkd->bkgt/dot_general | solution.py:45
  156.0 5.2 %fusion.50 = f32[512,8]{0,1:T(8,128)S(1)} fusion(f32[512,8,1152]{2,0,1:T(8,128)S(1)} %get-tuple-element.279, f32[512,8]{0,1:T(8,128)S(1)} %get-tuple-element.280, pred[512,1152]{1,0:T(8,128)(4,1)S(1)} %and_or_fusion.2), kind=kLoop, calls=%fused_computation.5.clone.1 | loop fusion | flops 18870272 | bytes 19496960 | tf_op jit(solution)/shard_map/while/body/eval_jaxpr/reduce_sum | solution.py:57
  161.3 5.0 %fusion.51 = bf16[1,128,512,8]{2,1,3,0:T(8,128)(2,1)S(1)} fusion(f32[512,8,1152]{2,0,1:T(8,128)S(1)} %get-tuple-element.279, f32[512,8]{0,1:T(8,128)S(1)} %get-tuple-element.280, pred[512,1152]{1,0:T(8,128)(4,1)S(1)} %and_or_fusion.2, f32[512,8]{0,1:T(8,128)S(1)} %fusion.50, bf16[1152,1,128]{0,2,1:T(8,128)(2,1)S(1)} %get-tuple-element.315), kind=kOutput, calls=%fused_computation.12.clone.1 | convolution fusion | flops 1227882496 | bytes 20840448 | tf_op jit(solution)/shard_map/while/body/eval_jaxpr/bkgt,tkd->bkgd/dot_general | solution.py:59
  171.7 4.6 %fusion.49 = (f32[512,8]{0,1:T(8,128)S(1)}, f32[512,8,1152]{2,0,1:T(8,128)S(1)}) fusion(pred[512,1152]{1,0:T(8,128)(4,1)S(1)} %and_or_fusion.2, bf16[512,8,128]{0,2,1:T(8,128)(2,1)S(1)} %bitcast.97, bf16[1152,1,128]{2,0,1:T(8,128)(2,1)S(1)} %get-tuple-element.314), kind=kOutput, calls=%fused_computation.4.clone.1 | convolution fusion | flops 1222111232 | bytes 20824064 | tf_op jit(solution)/shard_map/while/body/eval_jaxpr/bkgd,tkd->bkgt/dot_general | solution.py:45
  176.3 5.2 %fusion.50 = f32[512,8]{0,1:T(8,128)S(1)} fusion(f32[512,8,1152]{2,0,1:T(8,128)S(1)} %get-tuple-element.279, f32[512,8]{0,1:T(8,128)S(1)} %get-tuple-element.280, pred[512,1152]{1,0:T(8,128)(4,1)S(1)} %and_or_fusion.2), kind=kLoop, calls=%fused_computation.5.clone.1 | loop fusion | flops 18870272 | bytes 19496960 | tf_op jit(solution)/shard_map/while/body/eval_jaxpr/reduce_sum | solution.py:57
  181.6 5.0 %fusion.51 = bf16[1,128,512,8]{2,1,3,0:T(8,128)(2,1)S(1)} fusion(f32[512,8,1152]{2,0,1:T(8,128)S(1)} %get-tuple-element.279, f32[512,8]{0,1:T(8,128)S(1)} %get-tuple-element.280, pred[512,1152]{1,0:T(8,128)(4,1)S(1)} %and_or_fusion.2, f32[512,8]{0,1:T(8,128)S(1)} %fusion.50, bf16[1152,1,128]{0,2,1:T(8,128)(2,1)S(1)} %get-tuple-element.315), kind=kOutput, calls=%fused_computation.12.clone.1 | convolution fusion | flops 1227882496 | bytes 20840448 | tf_op jit(solution)/shard_map/while/body/eval_jaxpr/bkgt,tkd->bkgd/dot_general | solution.py:59
  188.2 12.4 %all_to_all.10 = f32[16,128,8]{1,2,0:T(8,128)S(1)} all-to-all(f32[16,128,8]{1,2,0:T(8,128)S(1)} %bitcast.103), channel_id=1, replica_groups=mesh['ctx'=16,'tensor'=8] {'ctx'}, dimensions={0} | all-to-all | bytes 131072 | tf_op jit(solution)/shard_map/all_to_all | solution.py:103
  200.6 4.5 %all-to-all-start = ((bf16[16,128,1024]{2,1,0:T(8,128)(2,1)}), bf16[16,128,1024]{2,1,0:T(8,128)(2,1)}, u32[]{:S(2)}, u32[]{:S(2)}) async-start(bf16[16,128,1024]{2,1,0:T(8,128)(2,1)} %bitcast.100), calls=%async_computation | async-start | bytes 8388608 | tf_op jit(solution)/shard_map/all_to_all | solution.py:100
  205.5 4.5 %mul.161 = f32[16,128,8,128]{3,2,1,0:T(8,128)} broadcast(f32[16,128,8]{2,1,0:T(8,128)S(1)} %copy.25), dimensions={0,1,2} | broadcast | bytes 8454144 | tf_op jit(solution)/shard_map/mul | solution.py:109
  210.1 9.3 %mul.162 = f32[16,128,1024]{2,1,0:T(8,128)} reshape(f32[16,128,8,128]{3,2,1,0:T(8,128)} %mul.161) | data formatting | bytes 16777216 | tf_op jit(solution)/shard_map/mul | solution.py:109
  219.5 42.9 %all-to-all-done = bf16[16,128,1024]{2,1,0:T(8,128)(2,1)} async-done(((bf16[16,128,1024]{2,1,0:T(8,128)(2,1)}), bf16[16,128,1024]{2,1,0:T(8,128)(2,1)}, u32[]{:S(2)}, u32[]{:S(2)}) %all-to-all-start) | async-done | bytes 4194336 | tf_op jit(solution)/shard_map/all_to_all | solution.py:100
  262.3 6.2 %multiply_reduce_fusion = f32[128,1024]{1,0:T(8,128)S(1)} fusion(f32[16,128,1024]{2,1,0:T(8,128)} %mul.162, bf16[16,128,1024]{2,1,0:T(8,128)(2,1)} %all-to-all-done), kind=kLoop, calls=%fused_computation.27 | loop fusion | flops 6160384 | bytes 13107200 | tf_op jit(solution)/shard_map/reduce_sum | solution.py:108
  (75 shorter events, 25.5 us)
Async XLA Ops:
  6.5 42.8 %copy-start = (bf16[8192,128]{1,0:T(8,128)(2,1)S(1)}, bf16[8192,128]{1,0:T(8,128)(2,1)}, u32[]{:S(2)}) copy-start(bf16[8192,128]{1,0:T(8,128)(2,1)} %param.13) | copy-start | bytes 6291460
  6.5 30.2 %all-gather.3.cloned.1.call-start = ((), (), s32[]{:S(2)}) async-start(), calls=%async_computation.2 | async-start | bytes 2359296 | tf_op jit(solution)/shard_map/all_gather | solution.py:72
  7.3 100.0 %all-gather.5.cloned.1.call-start = ((), (), s32[]{:S(2)}) async-start(), calls=%async_computation.3 | async-start | bytes 4456448 | tf_op jit(solution)/shard_map/all_gather | solution.py:94
  47.6 1.5 copy-start.2
  47.6 1.7 copy-start.4
  49.3 6.3 %copy-start.3 = (bf16[1024,128]{1,0:T(8,128)(2,1)S(1)}, bf16[1024,128]{1,0:T(8,128)(2,1)}, u32[]{:S(2)}) copy-start(bf16[1024,128]{1,0:T(8,128)(2,1)} %param.15) | copy-start | bytes 786436
  200.6 61.7 %all-to-all-start = ((bf16[16,128,1024]{2,1,0:T(8,128)(2,1)}), bf16[16,128,1024]{2,1,0:T(8,128)(2,1)}, u32[]{:S(2)}, u32[]{:S(2)}) async-start(bf16[16,128,1024]{2,1,0:T(8,128)(2,1)} %bitcast.100), calls=%async_computation | async-start | bytes 8388608 | tf_op jit(solution)/shard_map/all_to_all | solution.py:100
  262.3 7.2 %copy-start.1 = (bf16[8192,128]{1,0:T(8,128)(2,1)S(1)}, bf16[8192,128]{1,0:T(8,128)(2,1)}, u32[]{:S(2)}) copy-start(bf16[8192,128]{1,0:T(8,128)(2,1)} %param.13) | copy-start | bytes 6291460
Sparse Core Ops, SparseCore 0:
  9.1 27.6 all-gather.2
  49.2 57.9 all-gather.4
where the time goes:
time: 277 us; the launch traced here: 276 us
  waiting for transfers between devices  124 us (45%)
  matrix products  53 us (19%)
  other arithmetic  35.9 us (13%)
  local copies, waits for them, and re-layouts  29.8 us (11%)
  between operations  13.6 us (5%)
  blocking collectives  12.4 us (4%)
  starting transfers between devices  4.58 us (2%)
  loops' own time  2.89 us (1%)
    all_gather x1, waiting for transfers between devices, local(): all_queries = lax.all_gather(query, 'ctx', axis=0, tiled=True)  51.6 us
    all_to_all x1, waiting for transfers between devices, local(): lax.all_to_all(part.reshape(shards, rows, width), 'ctx', split_axis=0, co...  42.9 us
    all_gather x1, waiting for transfers between devices, local(): whole = lax.all_gather(hidden, 'tensor', axis=1, tiled=True)  29.1 us
    reduce_sum x4, other arithmetic, one_block(): total_p = jnp.sum(prob, axis=3)  21 us
    dot_general x4, matrix products, one_block(): jnp.einsum('bkgt,tkd->bkgd', prob_low, value_heads, preferred_element_typ...  20.1 us
    dot_general x4, matrix products, one_block(): jnp.einsum('bkgd,tkd->bkgt', rows_q, key_heads, preferred_element_type=jn...  18.3 us
    mul x2, local copies, waits for them, and re-layouts, local(): came_out.astype(jnp.float32).reshape(shards, rows, heads, head_dim)  13.8 us
    all_to_all x1, blocking collectives, local(): lax.all_to_all(lse.reshape(shards, rows, heads), 'ctx', split_axis=0, con...  12.4 us
  transfers between devices with their start and end apart: 3, of which 3 were waited for; matrix products, arithmetic and copies ran while one was open for 8% of the time, Pallas kernels for 0%

commit v1 on v0

v1 whole, which is shorter than its diff:
```python
import functools

import jax
import jax.numpy as jnp
import numpy as np
from jax import lax
from jax.experimental import pallas as pl
from jax.experimental.pallas import tpu as pltpu
from jax.sharding import PartitionSpec as P

HEAD_DIM = 128
ROWS = 128
FEAT = 1024
SLOTS = 1024
HEADS = 8
HALF = 4 * ROWS
TILE = 512
KEYS = 4 * SLOTS + 4 * ROWS
WIDTH = HEADS * HEAD_DIM + 2 * HEAD_DIM
SCALE = 1.0 / HEAD_DIM**0.5
EXP2 = SCALE / float(np.log(2.0))
LOW = -1e30
MESH = pl.DeviceIdType.MESH
NT = (((1,), (1,)), ((), ()))
F32, BF16 = jnp.float32, jnp.bfloat16


def rotary_tables():
    half = HEAD_DIM // 2
    freq = 500000.0 ** (-2.0 * np.arange(half) / HEAD_DIM)
    angle = (16384 + np.arange(2048))[:, None] * freq[None, :]
    cosine, sine = np.cos(angle), np.sin(angle)
    both = np.stack(
        [np.concatenate([cosine, cosine], 1), np.concatenate([-sine, sine], 1)]
    )
    both = both.reshape(2, 16, ROWS, HEAD_DIM).transpose(1, 0, 2, 3)
    return both.astype(np.float32)


def eye():
    row = lax.broadcasted_iota(jnp.int32, (ROWS, ROWS), 0)
    col = lax.broadcasted_iota(jnp.int32, (ROWS, ROWS), 1)
    return row == col


def to_row(column):
    return jnp.sum(jnp.where(eye(), column, 0.0), axis=0, keepdims=True)


def to_column(row):
    wide = jnp.broadcast_to(row, (ROWS, ROWS))
    return jnp.sum(jnp.where(eye(), wide, 0.0), axis=1, keepdims=True)


def tile_step(q, state, keys, values, bias=None):
    s = lax.dot_general(q, keys, NT, preferred_element_type=F32)
    if bias is not None:
        s = (s.reshape(4, ROWS, TILE) + bias[None]).reshape(HALF, TILE)
    top = jnp.max(s, axis=1, keepdims=True)
    if state is not None:
        top = jnp.maximum(state[0], top)
    p = jnp.exp2((s - top) * EXP2).astype(BF16)
    add = jnp.dot(p, values, preferred_element_type=F32)
    if state is None:
        return top, add
    return top, state[1] * jnp.exp2((state[0] - top) * EXP2) + add


def kernel(
    hid, gain, wq, wk, wv, ck, cv, lens, tab, out,
    w, hbuf, gbuf, tabv, ssq, rs, acc, kvraw, lensb, kp, vp, qbuf, pout, pin, lout, lin,
    wsem, lsem, hs, hr, ss, sr, ks, kr, ls, lr, os_, or_, qs, qr, ps, pr, es, er,
):
    ci, ti = lax.axis_index("ctx"), lax.axis_index("tensor")
    z, x = lax.div(ci, 4), lax.rem(ci, 4)
    y, c = lax.div(ti, 2), lax.rem(ti, 2)

    def at_y(d, other=False):
        core = 1 - c if other else c
        return 2 * lax.rem(y + d, 4) + core

    def at_x(d):
        return lax.rem(x + d, 4)

    def at_z(d):
        return lax.rem(z + d, 4)

    def x_dev(d):
        return (4 * z + at_x(d), ti)

    def z_dev(d):
        return (4 * at_z(d) + x, ti)

    def y_dev(d):
        return (ci, at_y(d))

    sib = (ci, at_y(0, True))
    sends = []

    def remote(src, dst, send_sem, recv_sem, device):
        return pltpu.make_async_remote_copy(
            src_ref=src, dst_ref=dst, send_sem=send_sem, recv_sem=recv_sem,
            device_id=device, device_id_type=MESH,
        )

    def send(*args):
        copy = remote(*args)
        copy.start()
        sends.append(copy)

    order = [at_y(0), at_y(0, True), at_y(3), at_y(1), at_y(3, True), at_y(1, True), at_y(2), at_y(2, True)]
    own_h = pltpu.make_async_copy(hid, hbuf.at[ti], lsem.at[0])
    own_h.start()
    load_gain = pltpu.make_async_copy(gain, gbuf, lsem.at[1])
    load_gain.start()

    barrier = pltpu.get_barrier_semaphore()
    peers = [(ci, lax.rem(ti + d, 8)) for d in range(1, 8)]
    peers += [x_dev(d) for d in (1, 2, 3)] + [z_dev(d) for d in (1, 2, 3)]
    for peer in peers:
        pl.semaphore_signal(barrier, inc=1, device_id=peer, device_id_type=MESH)

    w_loads = []
    for i, t in enumerate(order):
        rows = pl.ds(pl.multiple_of(t * FEAT, FEAT), FEAT)
        loads = [
            pltpu.make_async_copy(wq.at[rows], w.at[rows, pl.ds(0, FEAT)], wsem.at[i, 0]),
            pltpu.make_async_copy(wk.at[rows], w.at[rows, pl.ds(FEAT, 128)], wsem.at[i, 1]),
            pltpu.make_async_copy(wv.at[rows], w.at[rows, pl.ds(FEAT + 128, 128)], wsem.at[i, 2]),
        ]
        for load in loads:
            load.start()
        w_loads.append(loads)
    load_k = pltpu.make_async_copy(ck, kvraw.at[x, 0], lsem.at[2])
    load_k.start()
    load_v = pltpu.make_async_copy(cv, kvraw.at[x, 1], lsem.at[3])
    load_v.start()
    load_tab = pltpu.make_async_copy(tab.at[ci], tabv, lsem.at[4])
    load_tab.start()
    lensb[x] = jnp.full((8, 128), lens[0], jnp.int32)
    own_h.wait()
    wide = hbuf[ti].astype(F32)
    squares = jnp.sum(wide * wide, axis=1, keepdims=True)
    ssq[ti] = jnp.broadcast_to(to_row(jnp.broadcast_to(squares, (ROWS, ROWS))), (8, 128))

    pl.semaphore_wait(barrier, len(peers))

    top_half, low_half = pl.ds(0, 64), pl.ds(64, 64)

    def h_slot(t, part):
        return hbuf.at[t, part]

    for d in range(1, 8):
        send(ssq.at[ti], ssq.at[ti], ss.at[d], sr.at[d], (ci, lax.rem(ti + d, 8)))
    send(hid.at[top_half], h_slot(ti, top_half), hs.at[0], hr.at[0], y_dev(1))
    send(hid.at[low_half], h_slot(ti, low_half), hs.at[1], hr.at[1], y_dev(3))
    send(hid, hbuf.at[ti], hs.at[4], hr.at[4], sib)
    send(hid.at[low_half], h_slot(ti, low_half), hs.at[2], hr.at[2], y_dev(1))
    send(hid.at[top_half], h_slot(ti, top_half), hs.at[3], hr.at[3], y_dev(3))
    for d in (1, 2, 3):
        send(lensb.at[x], lensb.at[x], ls.at[d], lr.at[d], x_dev(d))
    send(ck, kvraw.at[x, 0], ks.at[0], kr.at[0], x_dev(1))
    send(cv, kvraw.at[x, 1], ks.at[1], kr.at[1], x_dev(3))
    send(cv, kvraw.at[x, 1], ks.at[2], kr.at[2], x_dev(1))
    send(ck, kvraw.at[x, 0], ks.at[3], kr.at[3], x_dev(3))

    def h_wait(i, t, part=None):
        ref = hbuf.at[t] if part is None else h_slot(t, part)
        remote(ref, ref, hs.at[i], hr.at[i], sib).wait_recv()

    def h_pass(i, t, part, device):
        send(h_slot(t, part), h_slot(t, part), hs.at[i], hr.at[i], device)

    def kv_wait(i, d, which):
        ref = kvraw.at[at_x(d), which]
        remote(ref, ref, ks.at[i], kr.at[i], sib).wait_recv()

    def kv_pass(i, d, which, device):
        ref = kvraw.at[at_x(d), which]
        send(ref, ref, ks.at[i], kr.at[i], device)

    load_gain.wait()
    for d in range(1, 8):
        ref = ssq.at[lax.rem(ti + 8 - d, 8)]
        remote(ref, ref, ss.at[d], sr.at[d], sib).wait_recv()
    total = jnp.sum(ssq[...], axis=0)
    inverse = lax.rsqrt(total * (1.0 / 8192.0) + 1e-5)
    rs[...] = jnp.broadcast_to(to_column(inverse[0:1, :]), (ROWS, ROWS))

    def project(i):
        t = order[i]
        for load in w_loads[i]:
            load.wait()
        g = gbuf[pl.ds(pl.multiple_of(t * 8, 8), 8), :]
        pieces = []
        for k in range(8):
            piece = hbuf[t, :, k * 128 : (k + 1) * 128].astype(F32)
            pieces.append((piece * rs[...] * g[k : k + 1, :]).astype(BF16))
        normed = jnp.concatenate(pieces, axis=1)
        rows = pl.ds(pl.multiple_of(t * FEAT, FEAT), FEAT)
        add = jnp.dot(normed, w[rows, :], preferred_element_type=F32)
        if i == 0:
            acc[...] = add
        else:
            acc[...] += add

    project(0)
    h_wait(4, order[1])
    project(1)
    h_wait(0, at_y(3), top_half)
    h_pass(5, at_y(3), top_half, y_dev(1))
    h_wait(1, at_y(1), low_half)
    h_pass(6, at_y(1), low_half, y_dev(3))
    h_pass(7, at_y(3), top_half, sib)
    h_pass(8, at_y(1), low_half, sib)
    h_wait(2, at_y(3), low_half)
    h_pass(9, at_y(3), low_half, sib)
    project(2)
    h_wait(3, at_y(1), top_half)
    h_pass(10, at_y(1), top_half, sib)
    project(3)
    kv_wait(0, 3, 0)
    kv_pass(4, 3, 0, x_dev(1))
    kv_wait(1, 1, 1)
    kv_pass(5, 1, 1, x_dev(3))
    h_wait(7, order[4], top_half)
    h_wait(9, order[4], low_half)
    project(4)
    h_wait(8, order[5], low_half)
    h_wait(10, order[5], top_half)
    project(5)

    def prepare(position, d):
        xi = at_x(d)
        valid_len = lensb[xi][0:1, :]

        @pl.loop(0, SLOTS // 128)
        def _(step):
            part = pl.ds(pl.multiple_of(step * 128, 128), 128)
            to = pl.ds(pl.multiple_of(position * SLOTS + step * 128, 128), 128)
            row = lax.broadcasted_iota(jnp.int32, (128, 128), 0) + step * 128
            valid = row < valid_len
            first = kvraw[xi, 0, 0:16, :].astype(F32)[0:1, :]
            kp[to, :] = jnp.where(valid, kvraw[xi, 0, part, :].astype(F32), first).astype(BF16)
            vp[to, 0:128] = jnp.where(valid, kvraw[xi, 1, part, :].astype(F32), 0.0).astype(BF16)
            vp[to, 128:256] = jnp.where(valid, 1.0, 0.0).astype(BF16)

    load_k.wait()
    load_v.wait()
    prepare(0, 0)
    vp[4 * SLOTS :, 128:256] = jnp.ones((4 * ROWS, 128), BF16)

    h_wait(5, at_y(2), top_half)
    h_pass(11, at_y(2), top_half, sib)
    h_wait(6, at_y(2), low_half)
    h_pass(12, at_y(2), low_half, sib)
    project(6)
    h_wait(11, order[7], top_half)
    h_wait(12, order[7], low_half)
    load_tab.wait()
    project(7)

    def rotate(piece):
        return (piece * tabv[0] + pltpu.roll(piece, 64, 1) * tabv[1]).astype(BF16)

    own_rows = pl.ds(pl.multiple_of(4 * SLOTS + x * ROWS, ROWS), ROWS)
    kp[own_rows, :] = rotate(acc[:, FEAT : FEAT + 128])
    vp[own_rows, 0:128] = acc[:, FEAT + 128 :].astype(BF16)
    for h in range(HEADS):
        qbuf[z, h // 4, (h % 4) * 128 : (h % 4 + 1) * 128, :] = rotate(acc[:, h * 128 : (h + 1) * 128])
        if h == 3:
            for d in (1, 3, 2):
                send(qbuf.at[z, 0], qbuf.at[z, 0], qs.at[d, 0], qr.at[d, 0], z_dev(d))
            for d in (1, 3, 2):
                rows = kp.at[own_rows]
                send(rows, rows, os_.at[d, 0], or_.at[d, 0], x_dev(d))
                rows = vp.at[own_rows, pl.ds(0, 128)]
                send(rows, rows, os_.at[d, 1], or_.at[d, 1], x_dev(d))
    for d in (2, 1, 3):
        send(qbuf.at[z, 1], qbuf.at[z, 1], qs.at[d, 1], qr.at[d, 1], z_dev(d))

    def own_bias(d):
        row = lax.broadcasted_iota(jnp.int32, (ROWS, TILE), 0)
        col = lax.broadcasted_iota(jnp.int32, (ROWS, TILE), 1)
        least = 128 * (4 * (z - at_z(d)) - x)
        return jnp.where(row - col >= least, 0.0, LOW)

    def finish(state, zi, half):
        top, both = state
        denominator = both[:, 128:]
        pout[zi, half] = (both[:, :128] / denominator).astype(BF16)
        lse = top * SCALE + jnp.log(denominator)
        rows = [to_row(lse[h * 128 : (h + 1) * 128]) for h in range(4)]
        lout[zi, half] = jnp.concatenate(rows + rows, axis=0)

    def tile(q, state, i, bias=None):
        rows = slice(i * TILE, (i + 1) * TILE)
        return tile_step(q, state, kp[rows, :], vp[rows, :], bias)

    for d in (1, 2, 3):
        ref = lensb.at[at_x(4 - d)]
        remote(ref, ref, ls.at[d], lr.at[d], sib).wait_recv()
    q = qbuf[z, 0]
    state = tile(q, None, 0)
    state = tile(q, state, 1)
    kv_wait(2, 3, 1)
    prepare(1, 3)
    state = tile(q, state, 2)
    state = tile(q, state, 3)
    kv_wait(3, 1, 0)
    prepare(2, 1)
    state = tile(q, state, 4)
    state = tile(q, state, 5)
    kv_wait(4, 2, 0)
    kv_wait(5, 2, 1)
    prepare(3, 2)
    state = tile(q, state, 6)
    state = tile(q, state, 7)
    for d in (1, 2, 3):
        rows = pl.ds(pl.multiple_of(4 * SLOTS + at_x(4 - d) * ROWS, ROWS), ROWS)
        ref = kp.at[rows]
        remote(ref, ref, os_.at[d, 0], or_.at[d, 0], sib).wait_recv()
        ref = vp.at[rows, pl.ds(0, 128)]
        remote(ref, ref, os_.at[d, 1], or_.at[d, 1], sib).wait_recv()
    state = tile(q, state, 8, own_bias(0))
    finish(state, z, 0)

    def back(d, half):
        zi = at_z(d)
        return [
            remote(pout.at[zi, half], pin.at[z, half], ps.at[d, half], pr.at[d, half], z_dev(d)),
            remote(lout.at[zi, half], lin.at[z, half], es.at[d, half], er.at[d, half], z_dev(d)),
        ]

    @pl.loop(1, 8)
    def _(u):
        half = lax.div(u, 4)
        v = u + half * (7 - 2 * u)
        d = v + lax.div(v, 2) * (5 - 2 * v)
        zi = at_z(d)

        @pl.when(d != 0)
        def _():
            ref = qbuf.at[zi, half]
            remote(ref, ref, qs.at[4 - d, half], qr.at[4 - d, half], sib).wait_recv()

        q = qbuf[zi, half]
        state = None
        for i in range(8):
            state = tile(q, state, i)
        finish(tile(q, state, 8, own_bias(d)), zi, half)

        @pl.when(d != 0)
        def _():
            for copy in back(d, half):
                copy.start()

    for half in range(2):
        for d in (1, 2, 3):
            ref = pin.at[at_z(4 - d), half]
            remote(ref, ref, ps.at[d, half], pr.at[d, half], sib).wait_recv()
            ref = lin.at[at_z(4 - d), half]
            remote(ref, ref, es.at[d, half], er.at[d, half], sib).wait_recv()
        logs = [lout[z, half]] + [lin[at_z(d), half] for d in (1, 2, 3)]
        top = functools.reduce(jnp.maximum, logs)
        weights = [jnp.exp(log - top) for log in logs]
        denominator = functools.reduce(jnp.add, weights)
        weights = [weight / denominator for weight in weights]
        for h in range(4):
            rows = slice(h * 128, (h + 1) * 128)
            total = None
            for d in range(4):
                part = pout[z, half, rows, :] if d == 0 else pin[at_z(d), half, rows, :]
                term = part.astype(F32) * to_column(weights[d][h : h + 1, :])
                total = term if total is None else total + term
            head = half * 4 + h
            out[:, head * 128 : (head + 1) * 128] = total.astype(BF16)

    for copy in sends:
        copy.wait_send()
    for half in range(2):
        for d in (1, 2, 3):
            for copy in back(d, half):
                copy.wait_send()


def local(hidden, norm_gain, w_query, w_key, w_value, cache_keys, cache_values, cache_lengths):
    anywhere = pl.BlockSpec(memory_space=pl.ANY)
    tables = jnp.asarray(rotary_tables())
    dma = pltpu.SemaphoreType.DMA
    return pl.pallas_call(
        kernel,
        out_shape=jax.ShapeDtypeStruct((ROWS, FEAT), BF16),
        in_specs=[anywhere] * 7 + [pl.BlockSpec(memory_space=pltpu.SMEM), anywhere],
        out_specs=pl.BlockSpec(memory_space=pltpu.VMEM),
        scratch_shapes=[
            pltpu.VMEM((8 * FEAT, WIDTH), BF16),
            pltpu.VMEM((8, ROWS, FEAT), BF16),
            pltpu.VMEM((64, 128), F32),
            pltpu.VMEM((2, ROWS, 128), F32),
            pltpu.VMEM((8, 8, 128), F32),
            pltpu.VMEM((ROWS, ROWS), F32),
            pltpu.VMEM((ROWS, WIDTH), F32),
            pltpu.VMEM((4, 2, SLOTS, 128), BF16),
            pltpu.VMEM((4, 8, 128), jnp.int32),
            pltpu.VMEM((KEYS, 128), BF16),
            pltpu.VMEM((KEYS, 256), BF16),
            pltpu.VMEM((4, 2, HALF, 128), BF16),
            pltpu.VMEM((4, 2, HALF, 128), BF16),
            pltpu.VMEM((4, 2, HALF, 128), BF16),
            pltpu.VMEM((4, 2, 8, 128), F32),
            pltpu.VMEM((4, 2, 8, 128), F32),
            dma((8, 3)), dma((5,)),
            dma((13,)), dma((13,)),
            dma((8,)), dma((8,)),
            dma((6,)), dma((6,)),
            dma((4,)), dma((4,)),
            dma((4, 2)), dma((4, 2)),
            dma((4, 2)), dma((4, 2)),
            dma((4, 2)), dma((4, 2)),
            dma((4, 2)), dma((4, 2)),
        ],
        compiler_params=pltpu.CompilerParams(
            collective_id=0, has_side_effects=True, vmem_limit_bytes=60 * 2**20
        ),
        name="star_query",
    )(
        hidden, norm_gain.reshape(64, 128), w_query, w_key, w_value,
        cache_keys, cache_values, cache_lengths, tables,
    )


def solution(mesh):
    placed = (
        P("ctx", "tensor"),
        P(),
        P(None, "tensor"),
        P(None, "tensor"),
        P(None, "tensor"),
        P("ctx", "tensor"),
        P("ctx", "tensor"),
        P("ctx"),
    )
    return jax.shard_map(
        local, mesh=mesh, in_specs=placed, out_specs=P("ctx", "tensor"), check_vma=False
    )
```

time: 277 us -> 60.4 us (0.22)
  waiting for transfers between devices: 124 us -> 0 us
  Pallas kernels: 0 us -> 57.9 us
  matrix products: 53 us -> 0 us
  other arithmetic: 35.9 us -> 0 us
  local copies, waits for them, and re-layouts: 29.8 us -> 1.67 us
  between operations: 13.6 us -> 0.66 us
  blocking collectives: 12.4 us -> 0 us
  starting transfers between devices: 4.58 us -> 0 us
  loops' own time: 2.89 us -> 0 us
    all_gather x2 -> x0, waiting for transfers between devices: 80.7 us -> none  [the longest x1 51.6 us: local(): all_queries = lax.all_gather(query, 'ctx', axis=0, tiled=True)]
    pallas_call x0 -> x1, Pallas kernels: none -> 57.9 us  [local(): pl.pallas_call(kernel, out_shape=jax.ShapeDtypeStruct((ROWS, FEAT), BF16)...]
    dot_general x11 -> x0, matrix products: 53 us -> none  [the longest x4 20.1 us: one_block(): jnp.einsum('bkgt,tkd->bkgd', prob_low, value_heads, preferred_element_typ...]
    all_to_all x1 -> x0, waiting for transfers between devices: 42.9 us -> none  [local(): lax.all_to_all(part.reshape(shards, rows, width), 'ctx', split_axis=0, co...]
    reduce_sum x7 -> x0, other arithmetic: 29.2 us -> none  [the longest x4 21 us: one_block(): total_p = jnp.sum(prob, axis=3)]
    mul x2 -> x0, local copies, waits for them, and re-layouts: 13.8 us -> none  [local(): came_out.astype(jnp.float32).reshape(shards, rows, heads, head_dim)]
    all_to_all x1 -> x0, blocking collectives: 12.4 us -> none  [local(): lax.all_to_all(lse.reshape(shards, rows, heads), 'ctx', split_axis=0, con...]
    dynamic_slice x8 -> x0, local copies, waits for them, and re-layouts: 7.52 us -> none  [the longest x4 5.19 us: one_block(): lax.dynamic_slice_in_dim(queries, begin, block, 0)]
  transfers between devices with their start and end apart: 3 -> 0, of which waited for: 3 -> 0; matrix products, arithmetic and copies ran while one was open for 8% -> 0% of each run, Pallas kernels for 0% -> 0%
where the time goes in v1:
time: 60.4 us; the launch traced here: 60.2 us
  Pallas kernels  57.9 us (96%)
  local copies, waits for them, and re-layouts  1.67 us (3%)
  between operations  0.66 us (1%)
    pallas_call x1, Pallas kernels, local(): pl.pallas_call(kernel, out_shape=jax.ShapeDtypeStruct((ROWS, FEAT), BF16)...  57.9 us
    unnamed x1, local copies, waits for them, and re-layouts  1.67 us

profile of v1, /device:TPU:0, one launch (start us, length us, event | category | flops | bytes accessed | tf_op | source)
XLA Modules:
  0.0 60.2 jit_solution(4061938537838110117)
XLA Ops:
  0.7 57.9 %star_query.1 = bf16[128,1024]{1,0:T(8,128)(2,1)} custom-call(bf16[128,1024]{1,0:T(8,128)(2,1)} %hid.1, f32[64,128]{1,0:T(8,128)} %bitcast.1, bf16[8192,1024]{1,0:T(8,128)(2,1)} %wq.1, bf16[8192,128]{1,0:T(8,128)(2,1)} %wk.1, bf16[8192,128]{1,0:T(8,128)(2,1)} %wv.1, bf16[1024,128]{1,0:T(8,128)(2,1)} %ck.1, bf16[1024,128]{1,0:T(8,128)(2,1)} %cv.1, ...), custom_call_target="tpu_custom_call" | custom-call | tf_op jit(solution)/shard_map/star_query/pallas_call | solution.py:391
  58.6 1.7 %copy.12 = bf16[128,1024]{1,0:T(8,128)(2,1)} copy(bf16[128,1024]{1,0:T(8,128)(2,1)} %star_query.1) | data formatting | bytes 524288

commit v2 on v1

--- a/solution.py
+++ b/solution.py
@@ -52,8 +52,11 @@
     return jnp.sum(jnp.where(eye(), wide, 0.0), axis=1, keepdims=True)
 
 
-def tile_step(q, state, keys, values, bias=None):
-    s = lax.dot_general(q, keys, NT, preferred_element_type=F32)
+def scores(q, keys):
+    return lax.dot_general(q, keys, NT, preferred_element_type=F32)
+
+
+def absorb(s, state, values, bias=None):
     if bias is not None:
         s = (s.reshape(4, ROWS, TILE) + bias[None]).reshape(HALF, TILE)
     top = jnp.max(s, axis=1, keepdims=True)
@@ -68,7 +71,7 @@
 
 def kernel(
     hid, gain, wq, wk, wv, ck, cv, lens, tab, out,
-    w, hbuf, gbuf, tabv, ssq, rs, acc, kvraw, lensb, kp, vp, qbuf, pout, pin, lout, lin,
+    w, hbuf, gbuf, tabv, ssq, rs, acc, kvraw, lensb, kp, vp, qbuf, pout, pin, lout, lin, mst, ost,
     wsem, lsem, hs, hr, ss, sr, ks, kr, ls, lr, os_, or_, qs, qr, ps, pr, es, er,
 ):
     ci, ti = lax.axis_index("ctx"), lax.axis_index("tensor")
@@ -145,31 +148,29 @@
 
     pl.semaphore_wait(barrier, len(peers))
 
-    top_half, low_half = pl.ds(0, 64), pl.ds(64, 64)
-
-    def h_slot(t, part):
-        return hbuf.at[t, part]
+    def h_ref(t, first, count):
+        return hbuf.at[t, :, pl.ds(256 * first, 256 * count)]
+
+    def h_send(i, t, first, count, device):
+        send(h_ref(t, first, count), h_ref(t, first, count), hs.at[i], hr.at[i], device)
+
+    def h_wait(i, t, first, count):
+        ref = h_ref(t, first, count)
+        remote(ref, ref, hs.at[i], hr.at[i], sib).wait_recv()
 
     for d in range(1, 8):
         send(ssq.at[ti], ssq.at[ti], ss.at[d], sr.at[d], (ci, lax.rem(ti + d, 8)))
-    send(hid.at[top_half], h_slot(ti, top_half), hs.at[0], hr.at[0], y_dev(1))
-    send(hid.at[low_half], h_slot(ti, low_half), hs.at[1], hr.at[1], y_dev(3))
-    send(hid, hbuf.at[ti], hs.at[4], hr.at[4], sib)
-    send(hid.at[low_half], h_slot(ti, low_half), hs.at[2], hr.at[2], y_dev(1))
-    send(hid.at[top_half], h_slot(ti, top_half), hs.at[3], hr.at[3], y_dev(3))
+    for k in range(4):
+        h_send(k, ti, k, 1, y_dev(1))
+        h_send(4 + k, ti, (k + 2) % 4, 1, y_dev(3))
+        if k == 0:
+            h_send(12, ti, 0, 4, sib)
     for d in (1, 2, 3):
         send(lensb.at[x], lensb.at[x], ls.at[d], lr.at[d], x_dev(d))
     send(ck, kvraw.at[x, 0], ks.at[0], kr.at[0], x_dev(1))
     send(cv, kvraw.at[x, 1], ks.at[1], kr.at[1], x_dev(3))
     send(cv, kvraw.at[x, 1], ks.at[2], kr.at[2], x_dev(1))
     send(ck, kvraw.at[x, 0], ks.at[3], kr.at[3], x_dev(3))
-
-    def h_wait(i, t, part=None):
-        ref = hbuf.at[t] if part is None else h_slot(t, part)
-        remote(ref, ref, hs.at[i], hr.at[i], sib).wait_recv()
-
-    def h_pass(i, t, part, device):
-        send(h_slot(t, part), h_slot(t, part), hs.at[i], hr.at[i], device)
 
     def kv_wait(i, d, which):
         ref = kvraw.at[at_x(d), which]
@@ -186,49 +187,6 @@
     total = jnp.sum(ssq[...], axis=0)
     inverse = lax.rsqrt(total * (1.0 / 8192.0) + 1e-5)
     rs[...] = jnp.broadcast_to(to_column(inverse[0:1, :]), (ROWS, ROWS))
-
-    def project(i):
-        t = order[i]
-        for load in w_loads[i]:
-            load.wait()
-        g = gbuf[pl.ds(pl.multiple_of(t * 8, 8), 8), :]
-        pieces = []
-        for k in range(8):
-            piece = hbuf[t, :, k * 128 : (k + 1) * 128].astype(F32)
-            pieces.append((piece * rs[...] * g[k : k + 1, :]).astype(BF16))
-        normed = jnp.concatenate(pieces, axis=1)
-        rows = pl.ds(pl.multiple_of(t * FEAT, FEAT), FEAT)
-        add = jnp.dot(normed, w[rows, :], preferred_element_type=F32)
-        if i == 0:
-            acc[...] = add
-        else:
-            acc[...] += add
-
-    project(0)
-    h_wait(4, order[1])
-    project(1)
-    h_wait(0, at_y(3), top_half)
-    h_pass(5, at_y(3), top_half, y_dev(1))
-    h_wait(1, at_y(1), low_half)
-    h_pass(6, at_y(1), low_half, y_dev(3))
-    h_pass(7, at_y(3), top_half, sib)
-    h_pass(8, at_y(1), low_half, sib)
-    h_wait(2, at_y(3), low_half)
-    h_pass(9, at_y(3), low_half, sib)
-    project(2)
-    h_wait(3, at_y(1), top_half)
-    h_pass(10, at_y(1), top_half, sib)
-    project(3)
-    kv_wait(0, 3, 0)
-    kv_pass(4, 3, 0, x_dev(1))
-    kv_wait(1, 1, 1)
-    kv_pass(5, 1, 1, x_dev(3))
-    h_wait(7, order[4], top_half)
-    h_wait(9, order[4], low_half)
-    project(4)
-    h_wait(8, order[5], low_half)
-    h_wait(10, order[5], top_half)
-    project(5)
 
     def prepare(position, d):
         xi = at_x(d)
@@ -245,20 +203,74 @@
             vp[to, 0:128] = jnp.where(valid, kvraw[xi, 1, part, :].astype(F32), 0.0).astype(BF16)
             vp[to, 128:256] = jnp.where(valid, 1.0, 0.0).astype(BF16)
 
+    def project(i, first=0, count=4):
+        t = order[i]
+        g = gbuf[pl.ds(pl.multiple_of(t * 8, 8), 8), :]
+        pieces = []
+        for k in range(2 * first, 2 * (first + count)):
+            piece = hbuf[t, :, k * 128 : (k + 1) * 128].astype(F32)
+            pieces.append((piece * rs[...] * g[k : k + 1, :]).astype(BF16))
+        normed = jnp.concatenate(pieces, axis=1)
+        rows = pl.ds(pl.multiple_of(t * FEAT + first * 256, 256), count * 256)
+        return jnp.dot(normed, w[rows, :], preferred_element_type=F32)
+
+    def loaded(*chunks):
+        for i in chunks:
+            for load in w_loads[i]:
+                load.wait()
+
+    left, right, far = at_y(3), at_y(1), at_y(2)
+    loaded(0, 1)
+    acc[...] = project(0)
+    h_wait(12, order[1], 0, 4)
+    acc[...] += project(1)
+    for k in (0, 1):
+        h_wait(k, left, k, 1)
+        h_send(8 + k, left, k, 1, y_dev(1))
+        h_wait(4 + k, right, 2 + k, 1)
+        h_send(10 + k, right, 2 + k, 1, y_dev(3))
+    h_send(13, left, 0, 2, sib)
+    h_send(14, right, 2, 2, sib)
+    loaded(2, 3)
+    acc[...] += project(2, 0, 2) + project(3, 2, 2)
+    h_wait(13, order[4], 0, 2)
+    h_wait(14, order[5], 2, 2)
+    loaded(4, 5)
+    acc[...] += project(4, 0, 2) + project(5, 2, 2)
+    for k in (2, 3):
+        h_wait(k, left, k, 1)
+        h_wait(4 + k, right, k - 2, 1)
+    h_send(15, left, 2, 2, sib)
+    h_send(16, right, 0, 2, sib)
+    acc[...] += project(2, 2, 2) + project(3, 0, 2)
+    kv_wait(0, 3, 0)
+    kv_pass(4, 3, 0, x_dev(1))
+    kv_wait(1, 1, 1)
+    kv_pass(5, 1, 1, x_dev(3))
+    h_wait(15, order[4], 2, 2)
+    h_wait(16, order[5], 0, 2)
+    acc[...] += project(4, 2, 2) + project(5, 0, 2)
+    h_wait(8, far, 0, 1)
+    h_send(17, far, 0, 1, sib)
+    h_wait(10, far, 2, 1)
+    h_send(18, far, 2, 1, sib)
+    loaded(6, 7)
+    acc[...] += project(6, 0, 1) + project(6, 2, 1)
     load_k.wait()
     load_v.wait()
     prepare(0, 0)
     vp[4 * SLOTS :, 128:256] = jnp.ones((4 * ROWS, 128), BF16)
-
-    h_wait(5, at_y(2), top_half)
-    h_pass(11, at_y(2), top_half, sib)
-    h_wait(6, at_y(2), low_half)
-    h_pass(12, at_y(2), low_half, sib)
-    project(6)
-    h_wait(11, order[7], top_half)
-    h_wait(12, order[7], low_half)
     load_tab.wait()
-    project(7)
+    h_wait(9, far, 1, 1)
+    h_send(19, far, 1, 1, sib)
+    h_wait(11, far, 3, 1)
+    h_send(20, far, 3, 1, sib)
+    h_wait(17, order[7], 0, 1)
+    h_wait(18, order[7], 2, 1)
+    acc[...] += project(6, 1, 1) + project(6, 3, 1) + project(7, 0, 1) + project(7, 2, 1)
+    h_wait(19, order[7], 1, 1)
+    h_wait(20, order[7], 3, 1)
+    acc[...] += project(7, 1, 1) + project(7, 3, 1)
 
     def rotate(piece):
         return (piece * tabv[0] + pltpu.roll(piece, 64, 1) * tabv[1]).astype(BF16)
@@ -266,18 +278,20 @@
     own_rows = pl.ds(pl.multiple_of(4 * SLOTS + x * ROWS, ROWS), ROWS)
     kp[own_rows, :] = rotate(acc[:, FEAT : FEAT + 128])
     vp[own_rows, 0:128] = acc[:, FEAT + 128 :].astype(BF16)
+    for d in (1, 3, 2):
+        rows = kp.at[own_rows]
+        send(rows, rows, os_.at[d, 0], or_.at[d, 0], x_dev(d))
+        rows = vp.at[own_rows, pl.ds(0, 128)]
+        send(rows, rows, os_.at[d, 1], or_.at[d, 1], x_dev(d))
+
+    def q_send(d, half):
+        send(qbuf.at[z, half], qbuf.at[z, half], qs.at[d, half], qr.at[d, half], z_dev(d))
+
     for h in range(HEADS):
         qbuf[z, h // 4, (h % 4) * 128 : (h % 4 + 1) * 128, :] = rotate(acc[:, h * 128 : (h + 1) * 128])
         if h == 3:
-            for d in (1, 3, 2):
-                send(qbuf.at[z, 0], qbuf.at[z, 0], qs.at[d, 0], qr.at[d, 0], z_dev(d))
-            for d in (1, 3, 2):
-                rows = kp.at[own_rows]
-                send(rows, rows, os_.at[d, 0], or_.at[d, 0], x_dev(d))
-                rows = vp.at[own_rows, pl.ds(0, 128)]
-                send(rows, rows, os_.at[d, 1], or_.at[d, 1], x_dev(d))
-    for d in (2, 1, 3):
-        send(qbuf.at[z, 1], qbuf.at[z, 1], qs.at[d, 1], qr.at[d, 1], z_dev(d))
+            q_send(1, 0)
+            q_send(3, 0)
 
     def own_bias(d):
         row = lax.broadcasted_iota(jnp.int32, (ROWS, TILE), 0)
@@ -293,37 +307,47 @@
         rows = [to_row(lse[h * 128 : (h + 1) * 128]) for h in range(4)]
         lout[zi, half] = jnp.concatenate(rows + rows, axis=0)
 
-    def tile(q, state, i, bias=None):
-        rows = slice(i * TILE, (i + 1) * TILE)
-        return tile_step(q, state, kp[rows, :], vp[rows, :], bias)
+    def run(q, state, tiles, bias=None):
+        def rows(i):
+            return slice(i * TILE, (i + 1) * TILE)
+
+        s = scores(q, kp[rows(tiles[0]), :])
+        for n, i in enumerate(tiles):
+            later = scores(q, kp[rows(tiles[n + 1]), :]) if n + 1 < len(tiles) else None
+            state = absorb(s, state, vp[rows(i), :], bias if i == 8 else None)
+            s = later
+        return state
+
+    def keep(half, state):
+        mst[half] = jnp.broadcast_to(state[0], (HALF, 128))
+        ost[half] = state[1]
+
+    def kept(half):
+        return mst[half][:, 0:1], ost[half]
 
     for d in (1, 2, 3):
         ref = lensb.at[at_x(4 - d)]
         remote(ref, ref, ls.at[d], lr.at[d], sib).wait_recv()
-    q = qbuf[z, 0]
-    state = tile(q, None, 0)
-    state = tile(q, state, 1)
     kv_wait(2, 3, 1)
     prepare(1, 3)
-    state = tile(q, state, 2)
-    state = tile(q, state, 3)
     kv_wait(3, 1, 0)
     prepare(2, 1)
-    state = tile(q, state, 4)
-    state = tile(q, state, 5)
+    keep(0, run(qbuf[z, 0], None, range(6)))
+    q_send(2, 0)
+    q_send(2, 1)
+    keep(1, run(qbuf[z, 1], None, range(6)))
+    q_send(1, 1)
+    q_send(3, 1)
     kv_wait(4, 2, 0)
     kv_wait(5, 2, 1)
     prepare(3, 2)
-    state = tile(q, state, 6)
-    state = tile(q, state, 7)
+    keep(0, run(qbuf[z, 0], kept(0), (6, 7)))
     for d in (1, 2, 3):
         rows = pl.ds(pl.multiple_of(4 * SLOTS + at_x(4 - d) * ROWS, ROWS), ROWS)
         ref = kp.at[rows]
         remote(ref, ref, os_.at[d, 0], or_.at[d, 0], sib).wait_recv()
         ref = vp.at[rows, pl.ds(0, 128)]
         remote(ref, ref, os_.at[d, 1], or_.at[d, 1], sib).wait_recv()
-    state = tile(q, state, 8, own_bias(0))
-    finish(state, z, 0)
 
     def back(d, half):
         zi = at_z(d)
@@ -332,28 +356,20 @@
             remote(lout.at[zi, half], lin.at[z, half], es.at[d, half], er.at[d, half], z_dev(d)),
         ]
 
-    @pl.loop(1, 8)
+    @pl.loop(0, 6)
     def _(u):
-        half = lax.div(u, 4)
-        v = u + half * (7 - 2 * u)
+        half = lax.div(u, 3)
+        v = 1 + u + half * (5 - 2 * u)
         d = v + lax.div(v, 2) * (5 - 2 * v)
         zi = at_z(d)
-
-        @pl.when(d != 0)
-        def _():
-            ref = qbuf.at[zi, half]
-            remote(ref, ref, qs.at[4 - d, half], qr.at[4 - d, half], sib).wait_recv()
-
-        q = qbuf[zi, half]
-        state = None
-        for i in range(8):
-            state = tile(q, state, i)
-        finish(tile(q, state, 8, own_bias(d)), zi, half)
-
-        @pl.when(d != 0)
-        def _():
-            for copy in back(d, half):
-                copy.start()
+        ref = qbuf.at[zi, half]
+        remote(ref, ref, qs.at[4 - d, half], qr.at[4 - d, half], sib).wait_recv()
+        finish(run(qbuf[zi, half], None, range(9), own_bias(d)), zi, half)
+        for copy in back(d, half):
+            copy.start()
+
+    finish(run(qbuf[z, 0], kept(0), (8,), own_bias(0)), z, 0)
+    finish(run(qbuf[z, 1], kept(1), (6, 7, 8), own_bias(0)), z, 1)
 
     for half in range(2):
         for d in (1, 2, 3):
@@ -410,8 +426,10 @@
             pltpu.VMEM((4, 2, HALF, 128), BF16),
             pltpu.VMEM((4, 2, 8, 128), F32),
             pltpu.VMEM((4, 2, 8, 128), F32),
+            pltpu.VMEM((2, HALF, 128), F32),
+            pltpu.VMEM((2, HALF, 256), F32),
             dma((8, 3)), dma((5,)),
-            dma((13,)), dma((13,)),
+            dma((21,)), dma((21,)),
             dma((8,)), dma((8,)),
             dma((6,)), dma((6,)),
             dma((4,)), dma((4,)),

time: 60.4 us -> 58.6 us (0.970)
  Pallas kernels: 57.9 us -> 56.1 us
    pallas_call x1, Pallas kernels: 57.9 us -> 56.1 us  [local(): pl.pallas_call(kernel, out_shape=jax.ShapeDtypeStruct((ROWS, FEAT), BF16)...]
where the time goes in v2:
time: 58.6 us; the launch traced here: 58.4 us
  Pallas kernels  56.1 us (96%)
  local copies, waits for them, and re-layouts  1.67 us (3%)
  between operations  0.66 us (1%)
    pallas_call x1, Pallas kernels, local(): pl.pallas_call(kernel, out_shape=jax.ShapeDtypeStruct((ROWS, FEAT), BF16)...  56.1 us
    unnamed x1, local copies, waits for them, and re-layouts  1.67 us

profile of v2, /device:TPU:0, one launch (start us, length us, event | category | flops | bytes accessed | tf_op | source)
XLA Modules:
  0.0 58.4 jit_solution(1572006144893039122)
XLA Ops:
  0.7 56.1 %star_query.1 = bf16[128,1024]{1,0:T(8,128)(2,1)} custom-call(bf16[128,1024]{1,0:T(8,128)(2,1)} %hid.1, f32[64,128]{1,0:T(8,128)} %bitcast.1, bf16[8192,1024]{1,0:T(8,128)(2,1)} %wq.1, bf16[8192,128]{1,0:T(8,128)(2,1)} %wk.1, bf16[8192,128]{1,0:T(8,128)(2,1)} %wv.1, bf16[1024,128]{1,0:T(8,128)(2,1)} %ck.1, bf16[1024,128]{1,0:T(8,128)(2,1)} %cv.1, ...), custom_call_target="tpu_custom_call" | custom-call | tf_op jit(solution)/shard_map/star_query/pallas_call | solution.py:407
  56.8 1.7 %copy.12 = bf16[128,1024]{1,0:T(8,128)(2,1)} copy(bf16[128,1024]{1,0:T(8,128)(2,1)} %star_query.1) | data formatting | bytes 524288

commit v3 on v2

--- a/solution.py
+++ b/solution.py
@@ -15,7 +15,7 @@
 HEADS = 8
 HALF = 4 * ROWS
 TILE = 512
-KEYS = 4 * SLOTS + 4 * ROWS
+KEYS = 4 * SLOTS + 2 * TILE
 WIDTH = HEADS * HEAD_DIM + 2 * HEAD_DIM
 SCALE = 1.0 / HEAD_DIM**0.5
 EXP2 = SCALE / float(np.log(2.0))
@@ -243,10 +243,6 @@
     h_send(15, left, 2, 2, sib)
     h_send(16, right, 0, 2, sib)
     acc[...] += project(2, 2, 2) + project(3, 0, 2)
-    kv_wait(0, 3, 0)
-    kv_pass(4, 3, 0, x_dev(1))
-    kv_wait(1, 1, 1)
-    kv_pass(5, 1, 1, x_dev(3))
     h_wait(15, order[4], 2, 2)
     h_wait(16, order[5], 0, 2)
     acc[...] += project(4, 2, 2) + project(5, 0, 2)
@@ -259,7 +255,9 @@
     load_k.wait()
     load_v.wait()
     prepare(0, 0)
-    vp[4 * SLOTS :, 128:256] = jnp.ones((4 * ROWS, 128), BF16)
+    vp[4 * SLOTS : 4 * SLOTS + TILE, 128:256] = jnp.ones((TILE, 128), BF16)
+    vp[4 * SLOTS + TILE :, :] = jnp.zeros((TILE, 256), BF16)
+    kp[4 * SLOTS + TILE :, :] = jnp.broadcast_to(kvraw[x, 0, 0:16, :].astype(F32)[0:1, :], (TILE, 128)).astype(BF16)
     load_tab.wait()
     h_wait(9, far, 1, 1)
     h_send(19, far, 1, 1, sib)
@@ -293,30 +291,41 @@
             q_send(1, 0)
             q_send(3, 0)
 
-    def own_bias(d):
+    def own_bias():
         row = lax.broadcasted_iota(jnp.int32, (ROWS, TILE), 0)
         col = lax.broadcasted_iota(jnp.int32, (ROWS, TILE), 1)
-        least = 128 * (4 * (z - at_z(d)) - x)
-        return jnp.where(row - col >= least, 0.0, LOW)
+        return jnp.where(row - col >= -128 * x, 0.0, LOW)
 
     def finish(state, zi, half):
         top, both = state
         denominator = both[:, 128:]
         pout[zi, half] = (both[:, :128] / denominator).astype(BF16)
-        lse = top * SCALE + jnp.log(denominator)
-        rows = [to_row(lse[h * 128 : (h + 1) * 128]) for h in range(4)]
-        lout[zi, half] = jnp.concatenate(rows + rows, axis=0)
-
-    def run(q, state, tiles, bias=None):
-        def rows(i):
-            return slice(i * TILE, (i + 1) * TILE)
-
-        s = scores(q, kp[rows(tiles[0]), :])
-        for n, i in enumerate(tiles):
-            later = scores(q, kp[rows(tiles[n + 1]), :]) if n + 1 < len(tiles) else None
-            state = absorb(s, state, vp[rows(i), :], bias if i == 8 else None)
+        tops = jnp.broadcast_to(top, (HALF, 128))
+        parts = [slice(h * 128, (h + 1) * 128) for h in range(4)]
+        top_rows = jnp.concatenate([to_row(tops[part]) for part in parts] * 2, axis=0)
+        sum_rows = jnp.concatenate([to_row(denominator[part]) for part in parts] * 2, axis=0)
+        lout[zi, half] = top_rows * SCALE + jnp.log(sum_rows)
+
+    def run(*units):
+        steps = [(unit, tile) for unit in units for tile in unit[2]]
+
+        def rows(tile):
+            return slice(tile * TILE, (tile + 1) * TILE) if isinstance(tile, int) else tile
+
+        def ahead(step):
+            unit, tile = step
+            return scores(unit[0], kp[rows(tile), :])
+
+        s = ahead(steps[0])
+        state = None
+        for n, (unit, tile) in enumerate(steps):
+            later = ahead(steps[n + 1]) if n + 1 < len(steps) else None
+            if n == 0 or steps[n - 1][0] is not unit:
+                state = unit[1]
+            state = absorb(s, state, vp[rows(tile), :], own_bias() if tile == 8 else None)
             s = later
-        return state
+            if n + 1 == len(steps) or steps[n + 1][0] is not unit:
+                unit[3](state)
 
     def keep(half, state):
         mst[half] = jnp.broadcast_to(state[0], (HALF, 128))
@@ -328,48 +337,76 @@
     for d in (1, 2, 3):
         ref = lensb.at[at_x(4 - d)]
         remote(ref, ref, ls.at[d], lr.at[d], sib).wait_recv()
+    kv_wait(0, 3, 0)
+    kv_pass(4, 3, 0, x_dev(1))
+    kv_wait(1, 1, 1)
+    kv_pass(5, 1, 1, x_dev(3))
     kv_wait(2, 3, 1)
     prepare(1, 3)
     kv_wait(3, 1, 0)
     prepare(2, 1)
-    keep(0, run(qbuf[z, 0], None, range(6)))
+    run((qbuf[z, 0], None, range(6), functools.partial(keep, 0)))
     q_send(2, 0)
     q_send(2, 1)
-    keep(1, run(qbuf[z, 1], None, range(6)))
+    run((qbuf[z, 1], None, range(6), functools.partial(keep, 1)))
     q_send(1, 1)
     q_send(3, 1)
+
+    def back(d, half):
+        zi = at_z(d)
+        return [
+            remote(pout.at[zi, half], pin.at[z, half], ps.at[d, half], pr.at[d, half], z_dev(d)),
+            remote(lout.at[zi, half], lin.at[z, half], es.at[d, half], er.at[d, half], z_dev(d)),
+        ]
+
+    def end(d, half):
+        def call(state):
+            finish(state, at_z(d), half)
+            for copy in back(d, half):
+                copy.start()
+
+        return call
+
+    def q_wait(d, half):
+        ref = qbuf.at[at_z(d), half]
+        remote(ref, ref, qs.at[4 - d, half], qr.at[4 - d, half], sib).wait_recv()
+
+    def last(d):
+        return pl.ds(pl.multiple_of(4 * SLOTS + TILE * lax.div(z + d, 4), TILE), TILE)
+
+    def unit(d, half):
+        return (qbuf[at_z(d), half], None, [*range(8), last(d)], end(d, half))
+
+    q_wait(1, 0)
+    q_wait(3, 0)
+    run(
+        (qbuf[at_z(1), 0], None, range(6), functools.partial(keep, 2)),
+        (qbuf[at_z(3), 0], None, range(6), functools.partial(keep, 3)),
+    )
     kv_wait(4, 2, 0)
     kv_wait(5, 2, 1)
     prepare(3, 2)
-    keep(0, run(qbuf[z, 0], kept(0), (6, 7)))
     for d in (1, 2, 3):
         rows = pl.ds(pl.multiple_of(4 * SLOTS + at_x(4 - d) * ROWS, ROWS), ROWS)
         ref = kp.at[rows]
         remote(ref, ref, os_.at[d, 0], or_.at[d, 0], sib).wait_recv()
         ref = vp.at[rows, pl.ds(0, 128)]
         remote(ref, ref, os_.at[d, 1], or_.at[d, 1], sib).wait_recv()
-
-    def back(d, half):
-        zi = at_z(d)
-        return [
-            remote(pout.at[zi, half], pin.at[z, half], ps.at[d, half], pr.at[d, half], z_dev(d)),
-            remote(lout.at[zi, half], lin.at[z, half], es.at[d, half], er.at[d, half], z_dev(d)),
-        ]
-
-    @pl.loop(0, 6)
-    def _(u):
-        half = lax.div(u, 3)
-        v = 1 + u + half * (5 - 2 * u)
-        d = v + lax.div(v, 2) * (5 - 2 * v)
-        zi = at_z(d)
-        ref = qbuf.at[zi, half]
-        remote(ref, ref, qs.at[4 - d, half], qr.at[4 - d, half], sib).wait_recv()
-        finish(run(qbuf[zi, half], None, range(9), own_bias(d)), zi, half)
-        for copy in back(d, half):
-            copy.start()
-
-    finish(run(qbuf[z, 0], kept(0), (8,), own_bias(0)), z, 0)
-    finish(run(qbuf[z, 1], kept(1), (6, 7, 8), own_bias(0)), z, 1)
+    run(
+        (qbuf[at_z(1), 0], kept(2), [6, 7, last(1)], end(1, 0)),
+        (qbuf[at_z(3), 0], kept(3), [6, 7, last(3)], end(3, 0)),
+    )
+    q_wait(2, 0)
+    q_wait(2, 1)
+    run(unit(2, 0), unit(2, 1))
+    q_wait(1, 1)
+    q_wait(3, 1)
+    run(unit(1, 1), unit(3, 1))
+
+    run(
+        (qbuf[z, 0], kept(0), [6, 7, 8], lambda state: finish(state, z, 0)),
+        (qbuf[z, 1], kept(1), [6, 7, 8], lambda state: finish(state, z, 1)),
+    )
 
     for half in range(2):
         for d in (1, 2, 3):
@@ -426,8 +463,8 @@
             pltpu.VMEM((4, 2, HALF, 128), BF16),
             pltpu.VMEM((4, 2, 8, 128), F32),
             pltpu.VMEM((4, 2, 8, 128), F32),
-            pltpu.VMEM((2, HALF, 128), F32),
-            pltpu.VMEM((2, HALF, 256), F32),
+            pltpu.VMEM((4, HALF, 128), F32),
+            pltpu.VMEM((4, HALF, 256), F32),
             dma((8, 3)), dma((5,)),
             dma((21,)), dma((21,)),
             dma((8,)), dma((8,)),

time: 58.6 us -> 56.4 us (0.962)
  Pallas kernels: 56.1 us -> 53.9 us
    pallas_call x1, Pallas kernels: 56.1 us -> 53.9 us  [local(): pl.pallas_call(kernel, out_shape=jax.ShapeDtypeStruct((ROWS, FEAT), BF16)...]
where the time goes in v3:
time: 56.4 us; the launch traced here: 56.2 us
  Pallas kernels  53.9 us (96%)
  local copies, waits for them, and re-layouts  1.67 us (3%)
  between operations  0.66 us (1%)
    pallas_call x1, Pallas kernels, local(): pl.pallas_call(kernel, out_shape=jax.ShapeDtypeStruct((ROWS, FEAT), BF16)...  53.9 us
    unnamed x1, local copies, waits for them, and re-layouts  1.67 us

profile of v3, /device:TPU:0, one launch (start us, length us, event | category | flops | bytes accessed | tf_op | source)
XLA Modules:
  0.0 56.2 jit_solution(15469426300663779322)
XLA Ops:
  0.7 53.9 %star_query.1 = bf16[128,1024]{1,0:T(8,128)(2,1)} custom-call(bf16[128,1024]{1,0:T(8,128)(2,1)} %hid.1, f32[64,128]{1,0:T(8,128)} %bitcast.1, bf16[8192,1024]{1,0:T(8,128)(2,1)} %wq.1, bf16[8192,128]{1,0:T(8,128)(2,1)} %wk.1, bf16[8192,128]{1,0:T(8,128)(2,1)} %wv.1, bf16[1024,128]{1,0:T(8,128)(2,1)} %ck.1, bf16[1024,128]{1,0:T(8,128)(2,1)} %cv.1, ...), custom_call_target="tpu_custom_call" | custom-call | tf_op jit(solution)/shard_map/star_query/pallas_call | solution.py:444
  54.6 1.7 %copy.12 = bf16[128,1024]{1,0:T(8,128)(2,1)} copy(bf16[128,1024]{1,0:T(8,128)(2,1)} %star_query.1) | data formatting | bytes 524288

commit v4 on v3

--- a/solution.py
+++ b/solution.py
@@ -188,20 +188,22 @@
     inverse = lax.rsqrt(total * (1.0 / 8192.0) + 1e-5)
     rs[...] = jnp.broadcast_to(to_column(inverse[0:1, :]), (ROWS, ROWS))
 
-    def prepare(position, d):
+    places = {0: 0, 3: 1, 1: 2, 2: 3}
+
+    def slots(d):
+        return slice(places[d] * SLOTS, (places[d] + 1) * SLOTS)
+
+    def mark(d):
+        row = lax.broadcasted_iota(jnp.int32, (SLOTS, 128), 0)
+        valid = row < lensb[at_x(d)][0:1, :]
+        vp[slots(d), 128:256] = jnp.where(valid, 1.0, 0.0).astype(BF16)
+
+    def prepare(d):
         xi = at_x(d)
-        valid_len = lensb[xi][0:1, :]
-
-        @pl.loop(0, SLOTS // 128)
-        def _(step):
-            part = pl.ds(pl.multiple_of(step * 128, 128), 128)
-            to = pl.ds(pl.multiple_of(position * SLOTS + step * 128, 128), 128)
-            row = lax.broadcasted_iota(jnp.int32, (128, 128), 0) + step * 128
-            valid = row < valid_len
-            first = kvraw[xi, 0, 0:16, :].astype(F32)[0:1, :]
-            kp[to, :] = jnp.where(valid, kvraw[xi, 0, part, :].astype(F32), first).astype(BF16)
-            vp[to, 0:128] = jnp.where(valid, kvraw[xi, 1, part, :].astype(F32), 0.0).astype(BF16)
-            vp[to, 128:256] = jnp.where(valid, 1.0, 0.0).astype(BF16)
+        valid = vp[slots(d), 128:256]
+        first = jnp.broadcast_to(kvraw[xi, 0, 0:16, :].astype(F32)[0:1, :], (SLOTS, 128)).astype(BF16)
+        kp[slots(d), :] = kvraw[xi, 0] * valid + first * (1 - valid)
+        vp[slots(d), 0:128] = kvraw[xi, 1] * valid
 
     def project(i, first=0, count=4):
         t = order[i]
@@ -224,6 +226,11 @@
     acc[...] = project(0)
     h_wait(12, order[1], 0, 4)
     acc[...] += project(1)
+    for d in (1, 2, 3):
+        ref = lensb.at[at_x(4 - d)]
+        remote(ref, ref, ls.at[d], lr.at[d], sib).wait_recv()
+    for d in range(4):
+        mark(d)
     for k in (0, 1):
         h_wait(k, left, k, 1)
         h_send(8 + k, left, k, 1, y_dev(1))
@@ -254,7 +261,7 @@
     acc[...] += project(6, 0, 1) + project(6, 2, 1)
     load_k.wait()
     load_v.wait()
-    prepare(0, 0)
+    prepare(0)
     vp[4 * SLOTS : 4 * SLOTS + TILE, 128:256] = jnp.ones((TILE, 128), BF16)
     vp[4 * SLOTS + TILE :, :] = jnp.zeros((TILE, 256), BF16)
     kp[4 * SLOTS + TILE :, :] = jnp.broadcast_to(kvraw[x, 0, 0:16, :].astype(F32)[0:1, :], (TILE, 128)).astype(BF16)
@@ -334,21 +341,20 @@
     def kept(half):
         return mst[half][:, 0:1], ost[half]
 
-    for d in (1, 2, 3):
-        ref = lensb.at[at_x(4 - d)]
-        remote(ref, ref, ls.at[d], lr.at[d], sib).wait_recv()
+    q_send(2, 0)
+    q_send(2, 1)
     kv_wait(0, 3, 0)
     kv_pass(4, 3, 0, x_dev(1))
     kv_wait(1, 1, 1)
     kv_pass(5, 1, 1, x_dev(3))
     kv_wait(2, 3, 1)
-    prepare(1, 3)
+    prepare(3)
     kv_wait(3, 1, 0)
-    prepare(2, 1)
-    run((qbuf[z, 0], None, range(6), functools.partial(keep, 0)))
-    q_send(2, 0)
-    q_send(2, 1)
-    run((qbuf[z, 1], None, range(6), functools.partial(keep, 1)))
+    prepare(1)
+    run(
+        (qbuf[z, 0], None, range(6), functools.partial(keep, 0)),
+        (qbuf[z, 1], None, range(6), functools.partial(keep, 1)),
+    )
     q_send(1, 1)
     q_send(3, 1)
 
@@ -359,11 +365,12 @@
             remote(lout.at[zi, half], lin.at[z, half], es.at[d, half], er.at[d, half], z_dev(d)),
         ]
 
-    def end(d, half):
+    def end(d, half, *returns):
         def call(state):
             finish(state, at_z(d), half)
-            for copy in back(d, half):
-                copy.start()
+            for which in returns:
+                for copy in back(*which):
+                    copy.start()
 
         return call
 
@@ -374,8 +381,8 @@
     def last(d):
         return pl.ds(pl.multiple_of(4 * SLOTS + TILE * lax.div(z + d, 4), TILE), TILE)
 
-    def unit(d, half):
-        return (qbuf[at_z(d), half], None, [*range(8), last(d)], end(d, half))
+    def unit(d, half, *returns):
+        return (qbuf[at_z(d), half], None, [*range(8), last(d)], end(d, half, *returns))
 
     q_wait(1, 0)
     q_wait(3, 0)
@@ -385,35 +392,33 @@
     )
     kv_wait(4, 2, 0)
     kv_wait(5, 2, 1)
-    prepare(3, 2)
+    prepare(2)
     for d in (1, 2, 3):
         rows = pl.ds(pl.multiple_of(4 * SLOTS + at_x(4 - d) * ROWS, ROWS), ROWS)
         ref = kp.at[rows]
         remote(ref, ref, os_.at[d, 0], or_.at[d, 0], sib).wait_recv()
         ref = vp.at[rows, pl.ds(0, 128)]
         remote(ref, ref, os_.at[d, 1], or_.at[d, 1], sib).wait_recv()
+    q_wait(2, 0)
+    q_wait(2, 1)
     run(
         (qbuf[at_z(1), 0], kept(2), [6, 7, last(1)], end(1, 0)),
-        (qbuf[at_z(3), 0], kept(3), [6, 7, last(3)], end(3, 0)),
-    )
-    q_wait(2, 0)
-    q_wait(2, 1)
-    run(unit(2, 0), unit(2, 1))
+        (qbuf[at_z(3), 0], kept(3), [6, 7, last(3)], end(3, 0, (1, 0), (3, 0))),
+        unit(2, 0),
+        unit(2, 1, (2, 0), (2, 1)),
+    )
     q_wait(1, 1)
     q_wait(3, 1)
-    run(unit(1, 1), unit(3, 1))
-
-    run(
-        (qbuf[z, 0], kept(0), [6, 7, 8], lambda state: finish(state, z, 0)),
-        (qbuf[z, 1], kept(1), [6, 7, 8], lambda state: finish(state, z, 1)),
-    )
-
-    for half in range(2):
+    run(unit(1, 1), unit(3, 1, (1, 1), (3, 1)))
+
+    def arrived(half):
         for d in (1, 2, 3):
             ref = pin.at[at_z(4 - d), half]
             remote(ref, ref, ps.at[d, half], pr.at[d, half], sib).wait_recv()
             ref = lin.at[at_z(4 - d), half]
             remote(ref, ref, es.at[d, half], er.at[d, half], sib).wait_recv()
+
+    def combine(half):
         logs = [lout[z, half]] + [lin[at_z(d), half] for d in (1, 2, 3)]
         top = functools.reduce(jnp.maximum, logs)
         weights = [jnp.exp(log - top) for log in logs]
@@ -428,6 +433,18 @@
                 total = term if total is None else total + term
             head = half * 4 + h
             out[:, head * 128 : (head + 1) * 128] = total.astype(BF16)
+
+    def end_first(state):
+        finish(state, z, 0)
+        combine(0)
+
+    arrived(0)
+    run(
+        (qbuf[z, 0], kept(0), [6, 7, 8], end_first),
+        (qbuf[z, 1], kept(1), [6, 7, 8], lambda state: finish(state, z, 1)),
+    )
+    arrived(1)
+    combine(1)
 
     for copy in sends:
         copy.wait_send()

time: 56.4 us -> 58.1 us (1.030)
  Pallas kernels: 53.9 us -> 55.6 us
    pallas_call x1, Pallas kernels: 53.9 us -> 55.6 us  [local(): pl.pallas_call(kernel, out_shape=jax.ShapeDtypeStruct((ROWS, FEAT), BF16)...]
where the time goes in v4:
time: 58.1 us; the launch traced here: 57.9 us
  Pallas kernels  55.6 us (96%)
  local copies, waits for them, and re-layouts  1.67 us (3%)
  between operations  0.66 us (1%)
    pallas_call x1, Pallas kernels, local(): pl.pallas_call(kernel, out_shape=jax.ShapeDtypeStruct((ROWS, FEAT), BF16)...  55.6 us
    unnamed x1, local copies, waits for them, and re-layouts  1.67 us

profile of v4, /device:TPU:0, one launch (start us, length us, event | category | flops | bytes accessed | tf_op | source)
XLA Modules:
  0.0 57.9 jit_solution(3250329606806026215)
XLA Ops:
  0.7 55.6 %star_query.1 = bf16[128,1024]{1,0:T(8,128)(2,1)} custom-call(bf16[128,1024]{1,0:T(8,128)(2,1)} %hid.1, f32[64,128]{1,0:T(8,128)} %bitcast.1, bf16[8192,1024]{1,0:T(8,128)(2,1)} %wq.1, bf16[8192,128]{1,0:T(8,128)(2,1)} %wk.1, bf16[8192,128]{1,0:T(8,128)(2,1)} %wv.1, bf16[1024,128]{1,0:T(8,128)(2,1)} %ck.1, bf16[1024,128]{1,0:T(8,128)(2,1)} %cv.1, ...), custom_call_target="tpu_custom_call" | custom-call | tf_op jit(solution)/shard_map/star_query/pallas_call | solution.py:461
  56.3 1.7 %copy.12 = bf16[128,1024]{1,0:T(8,128)(2,1)} copy(bf16[128,1024]{1,0:T(8,128)(2,1)} %star_query.1) | data formatting | bytes 524288

commit v5 on v4

--- a/solution.py
+++ b/solution.py
@@ -226,11 +226,6 @@
     acc[...] = project(0)
     h_wait(12, order[1], 0, 4)
     acc[...] += project(1)
-    for d in (1, 2, 3):
-        ref = lensb.at[at_x(4 - d)]
-        remote(ref, ref, ls.at[d], lr.at[d], sib).wait_recv()
-    for d in range(4):
-        mark(d)
     for k in (0, 1):
         h_wait(k, left, k, 1)
         h_send(8 + k, left, k, 1, y_dev(1))
@@ -259,6 +254,11 @@
     h_send(18, far, 2, 1, sib)
     loaded(6, 7)
     acc[...] += project(6, 0, 1) + project(6, 2, 1)
+    for d in (1, 2, 3):
+        ref = lensb.at[at_x(4 - d)]
+        remote(ref, ref, ls.at[d], lr.at[d], sib).wait_recv()
+    for d in range(4):
+        mark(d)
     load_k.wait()
     load_v.wait()
     prepare(0)
@@ -280,6 +280,16 @@
     def rotate(piece):
         return (piece * tabv[0] + pltpu.roll(piece, 64, 1) * tabv[1]).astype(BF16)
 
+    def q_send(d, half):
+        send(qbuf.at[z, half], qbuf.at[z, half], qs.at[d, half], qr.at[d, half], z_dev(d))
+
+    def q_store(h):
+        qbuf[z, h // 4, (h % 4) * 128 : (h % 4 + 1) * 128, :] = rotate(acc[:, h * 128 : (h + 1) * 128])
+
+    for h in range(4):
+        q_store(h)
+    q_send(1, 0)
+    q_send(3, 0)
     own_rows = pl.ds(pl.multiple_of(4 * SLOTS + x * ROWS, ROWS), ROWS)
     kp[own_rows, :] = rotate(acc[:, FEAT : FEAT + 128])
     vp[own_rows, 0:128] = acc[:, FEAT + 128 :].astype(BF16)
@@ -288,15 +298,8 @@
         send(rows, rows, os_.at[d, 0], or_.at[d, 0], x_dev(d))
         rows = vp.at[own_rows, pl.ds(0, 128)]
         send(rows, rows, os_.at[d, 1], or_.at[d, 1], x_dev(d))
-
-    def q_send(d, half):
-        send(qbuf.at[z, half], qbuf.at[z, half], qs.at[d, half], qr.at[d, half], z_dev(d))
-
-    for h in range(HEADS):
-        qbuf[z, h // 4, (h % 4) * 128 : (h % 4 + 1) * 128, :] = rotate(acc[:, h * 128 : (h + 1) * 128])
-        if h == 3:
-            q_send(1, 0)
-            q_send(3, 0)
+    for h in range(4, 8):
+        q_store(h)
 
     def own_bias():
         row = lax.broadcasted_iota(jnp.int32, (ROWS, TILE), 0)
@@ -319,9 +322,13 @@
         def rows(tile):
             return slice(tile * TILE, (tile + 1) * TILE) if isinstance(tile, int) else tile
 
+        queries = {}
+
         def ahead(step):
             unit, tile = step
-            return scores(unit[0], kp[rows(tile), :])
+            if id(unit) not in queries:
+                queries[id(unit)] = unit[0]() if callable(unit[0]) else unit[0]
+            return scores(queries[id(unit)], kp[rows(tile), :])
 
         s = ahead(steps[0])
         state = None
@@ -341,8 +348,6 @@
     def kept(half):
         return mst[half][:, 0:1], ost[half]
 
-    q_send(2, 0)
-    q_send(2, 1)
     kv_wait(0, 3, 0)
     kv_pass(4, 3, 0, x_dev(1))
     kv_wait(1, 1, 1)
@@ -353,7 +358,7 @@
     prepare(1)
     run(
         (qbuf[z, 0], None, range(6), functools.partial(keep, 0)),
-        (qbuf[z, 1], None, range(6), functools.partial(keep, 1)),
+        (qbuf[z, 1], None, range(4), functools.partial(keep, 1)),
     )
     q_send(1, 1)
     q_send(3, 1)
@@ -378,6 +383,14 @@
         ref = qbuf.at[at_z(d), half]
         remote(ref, ref, qs.at[4 - d, half], qr.at[4 - d, half], sib).wait_recv()
 
+    def q_pass(d, half, to):
+        ref = qbuf.at[at_z(d), half]
+        send(ref, ref, qs.at[2, half], qr.at[2, half], z_dev(to))
+
+    def q_far(half):
+        q_wait(2, half)
+        return qbuf[at_z(2), half]
+
     def last(d):
         return pl.ds(pl.multiple_of(4 * SLOTS + TILE * lax.div(z + d, 4), TILE), TILE)
 
@@ -386,10 +399,13 @@
 
     q_wait(1, 0)
     q_wait(3, 0)
+    q_pass(3, 0, 1)
     run(
         (qbuf[at_z(1), 0], None, range(6), functools.partial(keep, 2)),
         (qbuf[at_z(3), 0], None, range(6), functools.partial(keep, 3)),
     )
+    q_wait(1, 1)
+    q_pass(1, 1, 3)
     kv_wait(4, 2, 0)
     kv_wait(5, 2, 1)
     prepare(2)
@@ -399,15 +415,12 @@
         remote(ref, ref, os_.at[d, 0], or_.at[d, 0], sib).wait_recv()
         ref = vp.at[rows, pl.ds(0, 128)]
         remote(ref, ref, os_.at[d, 1], or_.at[d, 1], sib).wait_recv()
-    q_wait(2, 0)
-    q_wait(2, 1)
     run(
         (qbuf[at_z(1), 0], kept(2), [6, 7, last(1)], end(1, 0)),
         (qbuf[at_z(3), 0], kept(3), [6, 7, last(3)], end(3, 0, (1, 0), (3, 0))),
-        unit(2, 0),
-        unit(2, 1, (2, 0), (2, 1)),
-    )
-    q_wait(1, 1)
+        (functools.partial(q_far, 0), None, [*range(8), last(2)], end(2, 0)),
+        (functools.partial(q_far, 1), None, [*range(8), last(2)], end(2, 1, (2, 0), (2, 1))),
+    )
     q_wait(3, 1)
     run(unit(1, 1), unit(3, 1, (1, 1), (3, 1)))
 
@@ -441,7 +454,7 @@
     arrived(0)
     run(
         (qbuf[z, 0], kept(0), [6, 7, 8], end_first),
-        (qbuf[z, 1], kept(1), [6, 7, 8], lambda state: finish(state, z, 1)),
+        (qbuf[z, 1], kept(1), [4, 5, 6, 7, 8], lambda state: finish(state, z, 1)),
     )
     arrived(1)
     combine(1)

time: 58.1 us -> 57.2 us (0.985)
  Pallas kernels: 55.6 us -> 54.8 us
    pallas_call x1, Pallas kernels: 55.6 us -> 54.8 us  [local(): pl.pallas_call(kernel, out_shape=jax.ShapeDtypeStruct((ROWS, FEAT), BF16)...]
where the time goes in v5:
time: 57.2 us; the launch traced here: 57.1 us
  Pallas kernels  54.8 us (96%)
  local copies, waits for them, and re-layouts  1.67 us (3%)
  between operations  0.66 us (1%)
    pallas_call x1, Pallas kernels, local(): pl.pallas_call(kernel, out_shape=jax.ShapeDtypeStruct((ROWS, FEAT), BF16)...  54.8 us
    unnamed x1, local copies, waits for them, and re-layouts  1.67 us

profile of v5, /device:TPU:0, one launch (start us, length us, event | category | flops | bytes accessed | tf_op | source)
XLA Modules:
  0.0 57.1 jit_solution(10435665577473609245)
XLA Ops:
  0.7 54.8 %star_query.1 = bf16[128,1024]{1,0:T(8,128)(2,1)} custom-call(bf16[128,1024]{1,0:T(8,128)(2,1)} %hid.1, f32[64,128]{1,0:T(8,128)} %bitcast.1, bf16[8192,1024]{1,0:T(8,128)(2,1)} %wq.1, bf16[8192,128]{1,0:T(8,128)(2,1)} %wk.1, bf16[8192,128]{1,0:T(8,128)(2,1)} %wv.1, bf16[1024,128]{1,0:T(8,128)(2,1)} %ck.1, bf16[1024,128]{1,0:T(8,128)(2,1)} %cv.1, ...), custom_call_target="tpu_custom_call" | custom-call | tf_op jit(solution)/shard_map/star_query/pallas_call | solution.py:474
  55.4 1.7 %copy.12 = bf16[128,1024]{1,0:T(8,128)(2,1)} copy(bf16[128,1024]{1,0:T(8,128)(2,1)} %star_query.1) | data formatting | bytes 524288

commit v6 on v5

--- a/solution.py
+++ b/solution.py
@@ -286,10 +286,11 @@
     def q_store(h):
         qbuf[z, h // 4, (h % 4) * 128 : (h % 4 + 1) * 128, :] = rotate(acc[:, h * 128 : (h + 1) * 128])
 
-    for h in range(4):
-        q_store(h)
-    q_send(1, 0)
-    q_send(3, 0)
+    for half in range(2):
+        for h in range(4 * half, 4 * half + 4):
+            q_store(h)
+        q_send(1, half)
+        q_send(3, half)
     own_rows = pl.ds(pl.multiple_of(4 * SLOTS + x * ROWS, ROWS), ROWS)
     kp[own_rows, :] = rotate(acc[:, FEAT : FEAT + 128])
     vp[own_rows, 0:128] = acc[:, FEAT + 128 :].astype(BF16)
@@ -298,8 +299,6 @@
         send(rows, rows, os_.at[d, 0], or_.at[d, 0], x_dev(d))
         rows = vp.at[own_rows, pl.ds(0, 128)]
         send(rows, rows, os_.at[d, 1], or_.at[d, 1], x_dev(d))
-    for h in range(4, 8):
-        q_store(h)
 
     def own_bias():
         row = lax.broadcasted_iota(jnp.int32, (ROWS, TILE), 0)
@@ -322,13 +321,9 @@
         def rows(tile):
             return slice(tile * TILE, (tile + 1) * TILE) if isinstance(tile, int) else tile
 
-        queries = {}
-
         def ahead(step):
             unit, tile = step
-            if id(unit) not in queries:
-                queries[id(unit)] = unit[0]() if callable(unit[0]) else unit[0]
-            return scores(queries[id(unit)], kp[rows(tile), :])
+            return scores(unit[0], kp[rows(tile), :])
 
         s = ahead(steps[0])
         state = None
@@ -358,10 +353,8 @@
     prepare(1)
     run(
         (qbuf[z, 0], None, range(6), functools.partial(keep, 0)),
-        (qbuf[z, 1], None, range(4), functools.partial(keep, 1)),
-    )
-    q_send(1, 1)
-    q_send(3, 1)
+        (qbuf[z, 1], None, range(6), functools.partial(keep, 1)),
+    )
 
     def back(d, half):
         zi = at_z(d)
@@ -387,10 +380,6 @@
         ref = qbuf.at[at_z(d), half]
         send(ref, ref, qs.at[2, half], qr.at[2, half], z_dev(to))
 
-    def q_far(half):
-        q_wait(2, half)
-        return qbuf[at_z(2), half]
-
     def last(d):
         return pl.ds(pl.multiple_of(4 * SLOTS + TILE * lax.div(z + d, 4), TILE), TILE)
 
@@ -400,12 +389,12 @@
     q_wait(1, 0)
     q_wait(3, 0)
     q_pass(3, 0, 1)
+    q_wait(1, 1)
+    q_pass(1, 1, 3)
     run(
         (qbuf[at_z(1), 0], None, range(6), functools.partial(keep, 2)),
         (qbuf[at_z(3), 0], None, range(6), functools.partial(keep, 3)),
     )
-    q_wait(1, 1)
-    q_pass(1, 1, 3)
     kv_wait(4, 2, 0)
     kv_wait(5, 2, 1)
     prepare(2)
@@ -415,14 +404,16 @@
         remote(ref, ref, os_.at[d, 0], or_.at[d, 0], sib).wait_recv()
         ref = vp.at[rows, pl.ds(0, 128)]
         remote(ref, ref, os_.at[d, 1], or_.at[d, 1], sib).wait_recv()
+    q_wait(2, 0)
+    q_wait(2, 1)
     run(
-        (qbuf[at_z(1), 0], kept(2), [6, 7, last(1)], end(1, 0)),
-        (qbuf[at_z(3), 0], kept(3), [6, 7, last(3)], end(3, 0, (1, 0), (3, 0))),
-        (functools.partial(q_far, 0), None, [*range(8), last(2)], end(2, 0)),
-        (functools.partial(q_far, 1), None, [*range(8), last(2)], end(2, 1, (2, 0), (2, 1))),
+        (qbuf[at_z(1), 0], kept(2), [6, 7, last(1)], end(1, 0, (1, 0))),
+        (qbuf[at_z(3), 0], kept(3), [6, 7, last(3)], end(3, 0, (3, 0))),
+        unit(2, 0, (2, 0)),
+        unit(2, 1, (2, 1)),
     )
     q_wait(3, 1)
-    run(unit(1, 1), unit(3, 1, (1, 1), (3, 1)))
+    run(unit(1, 1, (1, 1)), unit(3, 1, (3, 1)))
 
     def arrived(half):
         for d in (1, 2, 3):
@@ -454,7 +445,7 @@
     arrived(0)
     run(
         (qbuf[z, 0], kept(0), [6, 7, 8], end_first),
-        (qbuf[z, 1], kept(1), [4, 5, 6, 7, 8], lambda state: finish(state, z, 1)),
+        (qbuf[z, 1], kept(1), [6, 7, 8], lambda state: finish(state, z, 1)),
     )
     arrived(1)
     combine(1)

time: 57.2 us -> 55.7 us (0.974)
  Pallas kernels: 54.8 us -> 53.2 us
    pallas_call x1, Pallas kernels: 54.8 us -> 53.2 us  [local(): pl.pallas_call(kernel, out_shape=jax.ShapeDtypeStruct((ROWS, FEAT), BF16)...]
where the time goes in v6:
time: 55.7 us; the launch traced here: 55.6 us
  Pallas kernels  53.2 us (96%)
  local copies, waits for them, and re-layouts  1.67 us (3%)
  between operations  0.66 us (1%)
    pallas_call x1, Pallas kernels, local(): pl.pallas_call(kernel, out_shape=jax.ShapeDtypeStruct((ROWS, FEAT), BF16)...  53.2 us
    unnamed x1, local copies, waits for them, and re-layouts  1.67 us

profile of v6, /device:TPU:0, one launch (start us, length us, event | category | flops | bytes accessed | tf_op | source)
XLA Modules:
  0.0 55.6 jit_solution(491788816178531366)
XLA Ops:
  0.7 53.2 %star_query.1 = bf16[128,1024]{1,0:T(8,128)(2,1)} custom-call(bf16[128,1024]{1,0:T(8,128)(2,1)} %hid.1, f32[64,128]{1,0:T(8,128)} %bitcast.1, bf16[8192,1024]{1,0:T(8,128)(2,1)} %wq.1, bf16[8192,128]{1,0:T(8,128)(2,1)} %wk.1, bf16[8192,128]{1,0:T(8,128)(2,1)} %wv.1, bf16[1024,128]{1,0:T(8,128)(2,1)} %ck.1, bf16[1024,128]{1,0:T(8,128)(2,1)} %cv.1, ...), custom_call_target="tpu_custom_call" | custom-call | tf_op jit(solution)/shard_map/star_query/pallas_call | solution.py:465
  53.9 1.7 %copy.12 = bf16[128,1024]{1,0:T(8,128)(2,1)} copy(bf16[128,1024]{1,0:T(8,128)(2,1)} %star_query.1) | data formatting | bytes 524288
